TPU v7x, 128 devices: a whole 4x4x4 slice. The times are simulated.
128 devices in a mesh: dp: 8 (over x, y_lo), ctx: 16 (over y_hi, z, core).
Axes of the slice: x: 4, y: 4 (y_hi: 2, y_lo: 2; y = y_hi * 2 + y_lo), z: 4, core: 2. Of those that a mesh axis runs over, the one named last changes fastest.
Arguments:
- hyena_q: bfloat16 [16384, 4096], P(('dp', 'ctx')), parts along dimension 0, may hold values from -6 to 6
- hyena_k: bfloat16 [16384, 4096], P(('dp', 'ctx')), parts along dimension 0, may hold values from -6 to 6
- hyena_v: bfloat16 [16384, 4096], P(('dp', 'ctx')), parts along dimension 0, may hold values from -6 to 6
- short_filter: float32 [3, 3, 4096], replicated, may hold values from -3.5 to 3.5
- residue: float32 [4096, 16], P('ctx'), may hold values from -0.0625 to 0.0625
- decay_rate: float32 [4096, 16], P('ctx'), may hold values from 0.00012207031 to 0.034
- att_query: bfloat16 [16384, 4096], P(('dp', 'ctx')), parts along dimension 0, may hold values from -32 to 32
- att_key: bfloat16 [16384, 4096], P(('dp', 'ctx')), parts along dimension 0, may hold values from -6 to 6
- att_value: bfloat16 [16384, 4096], P(('dp', 'ctx')), parts along dimension 0, may hold values from -6 to 6
Outputs:
- hyena_out: bfloat16 [16384, 4096], P(('dp', 'ctx')), parts along dimension 0
- att_out: bfloat16 [16384, 4096], P(('dp', 'ctx')), parts along dimension 0
There are 8 independent parts, one for each index of `dp`. A program takes and returns all parts, laid end to end along the dimension named above; an argument that names none is the same for every part. Nothing has to cross between parts.
All inputs are finite; a program needn't handle non-finite values.
Results may differ from a plain program's by a relative error of at most 0.0058.
Values may be sent and summed in bfloat16 or wider, within the bound.
A program may use at most 128 MiB of HBM per device.

v0:
```python
import math

import jax
import jax.numpy as jnp
from jax import lax
from jax.sharding import PartitionSpec as P

HEAD_DIM = 128


HIGHEST = lax.Precision.HIGHEST


def causal_taps(rim_rows, feature, tap_weights):
    values = feature.astype(jnp.float32)
    padded = jnp.concatenate([rim_rows, values], 0)
    length = values.shape[0]
    taps_count = tap_weights.shape[0]
    result = tap_weights[0] * padded[taps_count - 1 : taps_count - 1 + length]
    for offset in range(1, taps_count):
        result = (
            result
            + tap_weights[offset]
            * padded[taps_count - 1 - offset : taps_count - 1 - offset + length]
        )
    return result


def dft_tables(first_size, second_size):
    total_size = first_size * second_size
    outer = jnp.arange(first_size, dtype=jnp.int32)
    inner = jnp.arange(first_size // 2, dtype=jnp.int32)
    later = jnp.arange(second_size, dtype=jnp.int32)
    angle_one = (outer[:, None] * inner[None, :] % first_size).astype(jnp.float32) * (
        2.0 * math.pi / first_size
    )
    angle_two = (later[:, None] * later[None, :] % second_size).astype(jnp.float32) * (
        2.0 * math.pi / second_size
    )
    angle_twist = (outer[:, None] * later[None, :] % total_size).astype(jnp.float32) * (
        2.0 * math.pi / total_size
    )
    return (
        jnp.cos(angle_one),
        jnp.sin(angle_one),
        jnp.cos(angle_two),
        jnp.sin(angle_two),
        jnp.cos(angle_twist)[:, :, None],
        jnp.sin(angle_twist)[:, :, None],
    )


def forward_dft(signal, tables):
    cos_one, sin_one, cos_two, sin_two, cos_twist, sin_twist = tables
    part_re = jnp.einsum("kn,nmc->kmc", cos_one, signal, precision=HIGHEST)
    part_im = -jnp.einsum("kn,nmc->kmc", sin_one, signal, precision=HIGHEST)
    turned_re = part_re * cos_twist + part_im * sin_twist
    turned_im = part_im * cos_twist - part_re * sin_twist
    spec_re = jnp.einsum("kmc,mj->kjc", turned_re, cos_two, precision=HIGHEST) + jnp.einsum(
        "kmc,mj->kjc", turned_im, sin_two, precision=HIGHEST
    )
    spec_im = jnp.einsum("kmc,mj->kjc", turned_im, cos_two, precision=HIGHEST) - jnp.einsum(
        "kmc,mj->kjc", turned_re, sin_two, precision=HIGHEST
    )
    return (spec_re, spec_im)


def inverse_dft(spec_re, spec_im, tables, total_size):
    cos_one, sin_one, cos_two, sin_two, cos_twist, sin_twist = tables
    back_re = jnp.einsum("kjc,jm->kmc", spec_re, cos_two, precision=HIGHEST) - jnp.einsum(
        "kjc,jm->kmc", spec_im, sin_two, precision=HIGHEST
    )
    back_im = jnp.einsum("kjc,jm->kmc", spec_im, cos_two, precision=HIGHEST) + jnp.einsum(
        "kjc,jm->kmc", spec_re, sin_two, precision=HIGHEST
    )
    twist_re = back_re * cos_twist - back_im * sin_twist
    twist_im = back_im * cos_twist + back_re * sin_twist
    result = jnp.einsum("kn,kmc->nmc", cos_one, twist_re, precision=HIGHEST) - jnp.einsum(
        "kn,kmc->nmc", sin_one, twist_im, precision=HIGHEST
    )
    return result / total_size


def long_conv(product, residue, decay_rate):
    length, channels = product.shape
    block_width = min(128, channels)
    block_count = channels // block_width
    total_size = 2 * length
    low_bits = (total_size & -total_size).bit_length() - 1
    first_size = 2 ** (low_bits // 2)
    second_size = total_size // first_size
    half_first = first_size // 2
    tables = dft_tables(first_size, second_size)
    time_index = jnp.arange(length, dtype=jnp.float32)[:, None]

    def one_block(items):
        piece_in, residue_piece, rate_piece = items
        kernel = jnp.zeros((length, block_width), jnp.float32)
        for mode_index in range(residue_piece.shape[1]):
            kernel = kernel + residue_piece[:, mode_index] * jnp.exp(
                -rate_piece[:, mode_index] * time_index
            )
        signal = piece_in.astype(jnp.float32).reshape(half_first, second_size, block_width)
        signal_re, signal_im = forward_dft(signal, tables)
        kernel_re, kernel_im = forward_dft(
            kernel.reshape(half_first, second_size, block_width), tables
        )
        joint_re = signal_re * kernel_re - signal_im * kernel_im
        joint_im = signal_re * kernel_im + signal_im * kernel_re
        return inverse_dft(joint_re, joint_im, tables, total_size).reshape(length, block_width)

    blocks_in = product.reshape(length, block_count, block_width).transpose(1, 0, 2)
    residue_blocks = residue.reshape(block_count, block_width, residue.shape[1])
    rate_blocks = decay_rate.reshape(block_count, block_width, decay_rate.shape[1])
    results = lax.map(one_block, (blocks_in, residue_blocks, rate_blocks))
    return results.transpose(1, 0, 2).reshape(length, channels)


def attend(pieces):
    length = pieces[0].shape[0]
    head_count = pieces[0].shape[2]
    head_width = pieces[0].shape[3]
    query_all = pieces[0].reshape(length, head_count, head_width)
    key_all = pieces[1].reshape(length, head_count, head_width)
    value_all = pieces[2].reshape(length, head_count, head_width)
    block_rows = min(length, max(512, length // 8))
    score_scale = head_width ** (-0.5)
    out_blocks = []
    for block_index in range(length // block_rows):
        start_row = block_index * block_rows
        key_end = start_row + block_rows
        query_block = query_all[start_row:key_end]
        scores = (
            jnp.einsum(
                "qhd,khd->hqk", query_block, key_all[:key_end], preferred_element_type=jnp.float32
            )
            * score_scale
        )
        query_pos = start_row + jnp.arange(block_rows, dtype=jnp.int32)[:, None]
        key_pos = jnp.arange(key_end, dtype=jnp.int32)[None, :]
        scores = jnp.where((key_pos <= query_pos)[None, :, :], scores, -jnp.inf)
        row_max = jnp.max(scores, axis=2, keepdims=True)
        expo_scores = jnp.exp(scores - row_max)
        denominator = jnp.sum(expo_scores, axis=2)
        weights = expo_scores.astype(jnp.bfloat16)
        mixed_out = jnp.einsum(
            "hqk,khd->qhd", weights, value_all[:key_end], preferred_element_type=jnp.float32
        )
        mixed_out = mixed_out / denominator.T[:, :, None]
        out_blocks.append(mixed_out.astype(jnp.bfloat16))
    attended = jnp.concatenate(out_blocks, 0).reshape(length, 1, head_count, head_width)
    return lax.all_to_all(attended, "ctx", split_axis=0, concat_axis=1, tiled=True)


def local(
    hyena_q, hyena_k, hyena_v, short_filter, residue, decay_rate, att_query, att_key, att_value
):
    seq_rows = hyena_q.shape[0]
    devices = lax.axis_size("ctx")
    channels = hyena_q.shape[1] // devices
    rim_count = short_filter.shape[1] - 1
    relaid = (
        lax.all_to_all(hyena_q, "ctx", split_axis=1, concat_axis=0, tiled=True),
        lax.all_to_all(hyena_k, "ctx", split_axis=1, concat_axis=0, tiled=True),
        lax.all_to_all(hyena_v, "ctx", split_axis=1, concat_axis=0, tiled=True),
    )
    offset = lax.axis_index("ctx") * channels
    local_taps = lax.dynamic_slice_in_dim(short_filter, offset, channels, 2)
    zero_rim = jnp.zeros((rim_count, channels), jnp.float32)
    query_mix = causal_taps(zero_rim, relaid[0], local_taps[0])
    key_mix = causal_taps(zero_rim, relaid[1], local_taps[1])
    value_mix = causal_taps(zero_rim, relaid[2], local_taps[2])
    product = lax.optimization_barrier((key_mix * value_mix).astype(jnp.bfloat16))
    smoothed = lax.optimization_barrier(
        long_conv(product, residue, decay_rate).astype(jnp.bfloat16)
    )
    outgoing = (query_mix * smoothed.astype(jnp.float32)).astype(jnp.bfloat16)
    returned = lax.all_to_all(outgoing, "ctx", split_axis=0, concat_axis=1, tiled=True)
    head_groups = att_query.shape[1] // (devices * HEAD_DIM)
    query_four = att_query.reshape(seq_rows, devices, head_groups, HEAD_DIM)
    key_four = att_key.reshape(seq_rows, devices, head_groups, HEAD_DIM)
    value_four = att_value.reshape(seq_rows, devices, head_groups, HEAD_DIM)
    attended = attend(
        (
            lax.all_to_all(query_four, "ctx", split_axis=1, concat_axis=0, tiled=True),
            lax.all_to_all(key_four, "ctx", split_axis=1, concat_axis=0, tiled=True),
            lax.all_to_all(value_four, "ctx", split_axis=1, concat_axis=0, tiled=True),
        )
    )
    att_out = attended.reshape(seq_rows, att_query.shape[1])
    return (returned, att_out)


def solution(mesh):
    placed = (
        P(("dp", "ctx"), None),
        P(("dp", "ctx"), None),
        P(("dp", "ctx"), None),
        P(),
        P("ctx", None),
        P("ctx", None),
        P(("dp", "ctx"), None),
        P(("dp", "ctx"), None),
        P(("dp", "ctx"), None),
    )
    return jax.shard_map(
        local,
        mesh=mesh,
        in_specs=placed,
        out_specs=(P(("dp", "ctx"), None), P(("dp", "ctx"), None)),
        check_vma=False,
    )
```

profile of v0, /device:TPU:1, one launch (start us, length us, event | category | flops | bytes accessed | tf_op | source)
XLA Modules:
  0.0 340.2 jit_solution(16211065567886195051)
XLA Ops:
  0.6 2.4 copy.155
  3.0 9.5 %all-to-all-start.2 = ((bf16[128,16,256]{0,2,1:T(8,128)(2,1)}), bf16[128,16,256]{0,2,1:T(8,128)(2,1)S(1)}, u32[]{:S(2)}, u32[]{:S(2)}) async-start(bf16[128,16,256]{0,2,1:T(8,128)(2,1)} %bitcast.13), calls=%async_computation.2 | async-start | bytes 2097152 | tf_op jit(solution)/shard_map/all_to_all | solution.py:165
  13.8 15.9 %all-to-all-done.2 = bf16[128,16,256]{0,2,1:T(8,128)(2,1)S(1)} async-done(((bf16[128,16,256]{0,2,1:T(8,128)(2,1)}), bf16[128,16,256]{0,2,1:T(8,128)(2,1)S(1)}, u32[]{:S(2)}, u32[]{:S(2)}) %all-to-all-start.2) | async-done | bytes 1048608 | tf_op jit(solution)/shard_map/all_to_all | solution.py:165
  29.7 4.4 %all-to-all-start.1 = ((bf16[128,16,256]{0,2,1:T(8,128)(2,1)}), bf16[128,16,256]{0,2,1:T(8,128)(2,1)S(1)}, u32[]{:S(2)}, u32[]{:S(2)}) async-start(bf16[128,16,256]{0,2,1:T(8,128)(2,1)} %bitcast.7), calls=%async_computation.1 | async-start | bytes 2097152 | tf_op jit(solution)/shard_map/all_to_all | solution.py:164
  35.3 16.0 %all-to-all-done.1 = bf16[128,16,256]{0,2,1:T(8,128)(2,1)S(1)} async-done(((bf16[128,16,256]{0,2,1:T(8,128)(2,1)}), bf16[128,16,256]{0,2,1:T(8,128)(2,1)S(1)}, u32[]{:S(2)}, u32[]{:S(2)}) %all-to-all-start.1) | async-done | bytes 1048608 | tf_op jit(solution)/shard_map/all_to_all | solution.py:164
  52.3 4.4 %all-to-all-start = ((bf16[128,16,256]{0,2,1:T(8,128)(2,1)}), bf16[128,16,256]{0,2,1:T(8,128)(2,1)S(1)}, u32[]{:S(2)}, u32[]{:S(2)}) async-start(bf16[128,16,256]{0,2,1:T(8,128)(2,1)} %bitcast.1), calls=%async_computation | async-start | bytes 2097152 | tf_op jit(solution)/shard_map/all_to_all | solution.py:163
  56.6 1.6 copy.170
  63.1 10.8 %all-to-all-done = bf16[128,16,256]{0,2,1:T(8,128)(2,1)S(1)} async-done(((bf16[128,16,256]{0,2,1:T(8,128)(2,1)}), bf16[128,16,256]{0,2,1:T(8,128)(2,1)S(1)}, u32[]{:S(2)}, u32[]{:S(2)}) %all-to-all-start) | async-done | bytes 1048608 | tf_op jit(solution)/shard_map/all_to_all | solution.py:163
  74.9 4.4 %all-to-all-start.6 = ((bf16[128,16,2,128]{3,0,2,1:T(8,128)(2,1)}), bf16[128,16,2,128]{3,0,2,1:T(8,128)(2,1)S(1)}, u32[]{:S(2)}, u32[]{:S(2)}) async-start(bf16[128,16,2,128]{3,0,2,1:T(8,128)(2,1)} %copy.171), calls=%async_computation.6 | async-start | bytes 2097152 | tf_op jit(solution)/shard_map/all_to_all | solution.py:187
  79.4 1.6 copy.164
  82.4 1.6 copy.167
  85.3 1.6 iota_compare_fusion
  88.3 8.3 %all-to-all-done.6 = bf16[128,16,2,128]{3,0,2,1:T(8,128)(2,1)S(1)} async-done(((bf16[128,16,2,128]{3,0,2,1:T(8,128)(2,1)}), bf16[128,16,2,128]{3,0,2,1:T(8,128)(2,1)S(1)}, u32[]{:S(2)}, u32[]{:S(2)}) %all-to-all-start.6) | async-done | bytes 1048608 | tf_op jit(solution)/shard_map/all_to_all | solution.py:187
  96.6 4.4 %all-to-all-start.5 = ((bf16[128,16,2,128]{3,0,2,1:T(8,128)(2,1)}), bf16[128,16,2,128]{3,0,2,1:T(8,128)(2,1)S(1)}, u32[]{:S(2)}, u32[]{:S(2)}) async-start(bf16[128,16,2,128]{3,0,2,1:T(8,128)(2,1)} %copy.168), calls=%async_computation.5 | async-start | bytes 2097152 | tf_op jit(solution)/shard_map/all_to_all | solution.py:186
  102.5 3.0 copy.156
  107.1 2.9 copy.154
  110.0 6.2 %multiply_convert_fusion.1 = bf16[2048,256]{1,0:T(8,128)(2,1)S(1)} fusion(f32[2048,256]{1,0:T(8,128)} %bitcast.355, f32[2048,256]{1,0:T(8,128)} %bitcast.356, f32[256]{0:T(256)S(1)} %bitcast.392, f32[256]{0:T(256)S(1)} %bitcast.387, f32[256]{0:T(256)S(1)} %bitcast.388, f32[256]{0:T(256)S(1)} %bitcast.389, f32[256]{0:T(256)S(1)} %bitcast.390, ...), kind=kLoop, calls=%fused_computation.271 | loop fusion | flops 6291456 | bytes 5249024 | tf_op jit(solution)/shard_map/convert_element_type | solution.py:173
  118.2 6.0 %all-to-all-start.4 = ((bf16[128,16,2,128]{3,0,2,1:T(8,128)(2,1)}), bf16[128,16,2,128]{3,0,2,1:T(8,128)(2,1)}, u32[]{:S(2)}, u32[]{:S(2)}) async-start(bf16[128,16,2,128]{3,0,2,1:T(8,128)(2,1)} %copy.165), calls=%async_computation.4 | async-start | bytes 2097152 | tf_op jit(solution)/shard_map/all_to_all | solution.py:185
  124.2 136.2 %while.12 = (s32[]{:T(128)}, bf16[2,2048,128]{1,2,0:T(8,128)(2,1)}, bf16[2,2048,128]{1,2,0:T(8,128)(2,1)S(1)}, f32[2,128,16]{1,0,2:T(2,128)S(1)}, f32[2,128,16]{1,0,2:T(2,128)S(1)}, /*index=5*/s32[]{:T(128)}) while((s32[]{:T(128)}, bf16[2,2048,128]{1,2,0:T(8,128)(2,1)}, bf16[2,2048,128]{1,2,0:T(8,128)(2,1)S(1)}, ...), condition=%wide.region_1.2_spmd.clone.clone, body=%wide.region_0.1_spmd.clone.clone.sunk | while | flops 6082926592 | bytes 143433952 | solution.py:115
  124.7 8.7 %fusion.385 = f32[64,128,64]{1,2,0:T(8,128)} fusion(f32[128]{0:T(128)S(1)} %get-tuple-element.457, f32[128]{0:T(128)S(1)} %get-tuple-element.459, f32[128]{0:T(128)S(1)} %get-tuple-element.460, f32[128]{0:T(128)S(1)} %get-tuple-element.461, f32[128]{0:T(128)S(1)} %get-tuple-element.462, f32[128]{0:T(128)S(1)} %get-tuple-element.463, ...), kind=kOutput, calls=%fused_computation.105.clone.1 | convolution fusion | flops 213676032 | bytes 2121728 | tf_op jit(solution)/shard_map/while/body/eval_jaxpr/kn,nmc->kmc/dot_general | solution.py:56
  136.1 5.2 %fusion.388 = (f32[64,64,128]{2,0,1:T(8,128)S(1)}, f32[64,64,128]{2,0,1:T(8,128)S(1)}, f32[64,64,128]{2,0,1:T(8,128)S(1)}, f32[64,64,128]{2,0,1:T(8,128)S(1)}) fusion(f32[64,128,64]{1,2,0:T(8,128)S(1)} %copy-done.30, f32[64,64]{0,1:T(8,128)S(1)} %get-tuple-element.490, f32[64,64]{0,1:T(8,128)S(1)} %get-tuple-element.491, ...), kind=kOutput, calls=%fused_computation.17.clone.1 | convolution fusion | flops 221016064 | bytes 14737408 | tf_op jit(solution)/shard_map/while/body/eval_jaxpr/kn,nmc->kmc/dot_general | solution.py:55
  141.3 3.3 fusion.389
  144.6 3.5 %fusion.390 = f32[64,128,64]{1,2,0:T(8,128)S(1)} fusion(f32[64,128,64]{1,2,0:T(8,128)S(1)} %fusion.389, f32[64,64,128]{2,0,1:T(8,128)S(1)} %get-tuple-element.493), kind=kOutput, calls=%fused_computation.54.clone.1 | convolution fusion | flops 403234816 | bytes 6291456 | tf_op jit(solution)/shard_map/while/body/eval_jaxpr/kmc,mj->kjc/dot_general | solution.py:62
  148.1 3.3 fusion.391
  151.5 3.3 fusion.392
  154.8 3.8 %fusion.393 = f32[64,128,64]{1,2,0:T(8,128)S(1)} fusion(f32[64,64,128]{2,0,1:T(8,128)S(1)} %get-tuple-element.492), kind=kOutput, calls=%fused_computation.37.clone.1 | convolution fusion | flops 402710528 | bytes 4194304 | tf_op jit(solution)/shard_map/while/body/eval_jaxpr/kmc,mj->kjc/dot_general | solution.py:59
  158.6 3.3 fusion.394
  161.9 3.3 fusion.395
  165.2 4.0 %multiply_subtract_fusion.2 = (f32[64,128,64]{1,2,0:T(8,128)S(1)}, f32[64,128,64]{1,2,0:T(8,128)S(1)}) fusion(f32[64,128,64]{1,2,0:T(8,128)S(1)} %fusion.390, f32[64,128,64]{1,2,0:T(8,128)S(1)} %fusion.392, f32[64,128,64]{1,2,0:T(8,128)S(1)} %fusion.394, f32[64,128,64]{1,2,0:T(8,128)S(1)} %fusion.395, f32[64,64,128]{2,0,1:T(8,128)S(1)} %get-tuple-element.495), kind=kOutput, calls=%fused_computation.34.clone.1 | convolution fusion | flops 406380544 | bytes 14680064 | tf_op jit(solution)/shard_map/while/body/eval_jaxpr/kmc,mj->kjc/dot_general | solution.py:62
  169.2 2.3 fusion.396
  171.5 3.4 %fusion.397 = f32[64,128,64]{1,2,0:T(8,128)} fusion(f32[64,128,64]{1,2,0:T(8,128)S(1)} %fusion.396, f32[64,128,64]{1,2,0:T(8,128)S(1)} %get-tuple-element.497), kind=kOutput, calls=%fused_computation.55.clone.1 | convolution fusion | flops 403234816 | bytes 6291456 | tf_op jit(solution)/shard_map/while/body/eval_jaxpr/kjc,jm->kmc/dot_general | solution.py:70
  175.1 3.8 %fusion.398 = f32[64,128,64]{1,2,0:T(8,128)S(1)} fusion(f32[64,128,64]{1,2,0:T(8,128)} %copy-done), kind=kOutput, calls=%fused_computation.7.clone.1 | convolution fusion | flops 402710528 | bytes 4194304 | tf_op jit(solution)/shard_map/while/body/eval_jaxpr/kjc,jm->kmc/dot_general | solution.py:73
  179.0 3.3 subtract_bitcast_fusion.2
  182.3 2.5 fusion.399
  184.8 2.5 fusion.400
  189.2 8.6 %fusion.385 = f32[64,128,64]{1,2,0:T(8,128)} fusion(f32[128]{0:T(128)S(1)} %get-tuple-element.457, f32[128]{0:T(128)S(1)} %get-tuple-element.459, f32[128]{0:T(128)S(1)} %get-tuple-element.460, f32[128]{0:T(128)S(1)} %get-tuple-element.461, f32[128]{0:T(128)S(1)} %get-tuple-element.462, f32[128]{0:T(128)S(1)} %get-tuple-element.463, ...), kind=kOutput, calls=%fused_computation.105.clone.1 | convolution fusion | flops 213676032 | bytes 2121728 | tf_op jit(solution)/shard_map/while/body/eval_jaxpr/kn,nmc->kmc/dot_general | solution.py:56
  200.5 5.2 %fusion.388 = (f32[64,64,128]{2,0,1:T(8,128)S(1)}, f32[64,64,128]{2,0,1:T(8,128)S(1)}, f32[64,64,128]{2,0,1:T(8,128)S(1)}, f32[64,64,128]{2,0,1:T(8,128)S(1)}) fusion(f32[64,128,64]{1,2,0:T(8,128)S(1)} %copy-done.30, f32[64,64]{0,1:T(8,128)S(1)} %get-tuple-element.490, f32[64,64]{0,1:T(8,128)S(1)} %get-tuple-element.491, ...), kind=kOutput, calls=%fused_computation.17.clone.1 | convolution fusion | flops 221016064 | bytes 14737408 | tf_op jit(solution)/shard_map/while/body/eval_jaxpr/kn,nmc->kmc/dot_general | solution.py:55
  205.7 3.3 fusion.389
  209.0 3.5 %fusion.390 = f32[64,128,64]{1,2,0:T(8,128)S(1)} fusion(f32[64,128,64]{1,2,0:T(8,128)S(1)} %fusion.389, f32[64,64,128]{2,0,1:T(8,128)S(1)} %get-tuple-element.493), kind=kOutput, calls=%fused_computation.54.clone.1 | convolution fusion | flops 403234816 | bytes 6291456 | tf_op jit(solution)/shard_map/while/body/eval_jaxpr/kmc,mj->kjc/dot_general | solution.py:62
  212.5 3.3 fusion.391
  215.9 3.3 fusion.392
  219.2 3.8 %fusion.393 = f32[64,128,64]{1,2,0:T(8,128)S(1)} fusion(f32[64,64,128]{2,0,1:T(8,128)S(1)} %get-tuple-element.492), kind=kOutput, calls=%fused_computation.37.clone.1 | convolution fusion | flops 402710528 | bytes 4194304 | tf_op jit(solution)/shard_map/while/body/eval_jaxpr/kmc,mj->kjc/dot_general | solution.py:59
  222.9 3.3 fusion.394
  226.3 3.3 fusion.395
  229.6 4.0 %multiply_subtract_fusion.2 = (f32[64,128,64]{1,2,0:T(8,128)S(1)}, f32[64,128,64]{1,2,0:T(8,128)S(1)}) fusion(f32[64,128,64]{1,2,0:T(8,128)S(1)} %fusion.390, f32[64,128,64]{1,2,0:T(8,128)S(1)} %fusion.392, f32[64,128,64]{1,2,0:T(8,128)S(1)} %fusion.394, f32[64,128,64]{1,2,0:T(8,128)S(1)} %fusion.395, f32[64,64,128]{2,0,1:T(8,128)S(1)} %get-tuple-element.495), kind=kOutput, calls=%fused_computation.34.clone.1 | convolution fusion | flops 406380544 | bytes 14680064 | tf_op jit(solution)/shard_map/while/body/eval_jaxpr/kmc,mj->kjc/dot_general | solution.py:62
  233.6 2.3 fusion.396
  235.9 3.4 %fusion.397 = f32[64,128,64]{1,2,0:T(8,128)} fusion(f32[64,128,64]{1,2,0:T(8,128)S(1)} %fusion.396, f32[64,128,64]{1,2,0:T(8,128)S(1)} %get-tuple-element.497), kind=kOutput, calls=%fused_computation.55.clone.1 | convolution fusion | flops 403234816 | bytes 6291456 | tf_op jit(solution)/shard_map/while/body/eval_jaxpr/kjc,jm->kmc/dot_general | solution.py:70
  239.5 3.8 %fusion.398 = f32[64,128,64]{1,2,0:T(8,128)S(1)} fusion(f32[64,128,64]{1,2,0:T(8,128)} %copy-done), kind=kOutput, calls=%fused_computation.7.clone.1 | convolution fusion | flops 402710528 | bytes 4194304 | tf_op jit(solution)/shard_map/while/body/eval_jaxpr/kjc,jm->kmc/dot_general | solution.py:73
  243.4 3.3 subtract_bitcast_fusion.2
  246.7 2.5 fusion.399
  249.2 2.5 fusion.400
  260.4 2.5 copy.181
  270.2 1.9 copy.152
  272.1 3.0 multiply_convert_fusion
  275.1 7.2 %all-to-all-start.3 = ((bf16[16,128,256]{2,1,0:T(8,128)(2,1)}), bf16[16,128,256]{2,1,0:T(8,128)(2,1)S(1)}, u32[]{:S(2)}, u32[]{:S(2)}) async-start(bf16[16,128,256]{2,1,0:T(8,128)(2,1)} %bitcast.364), calls=%async_computation.3 | async-start | bytes 2097152 | tf_op jit(solution)/shard_map/all_to_all | solution.py:178
  285.6 1.9 fusion.225
  287.5 2.5 fusion.226
  289.9 2.6 fusion.265
  294.0 2.1 fusion.229
  301.5 2.1 fusion.271
  303.7 9.5 %copy.183 = bf16[2048,1,2,128]{3,2,1,0:T(2,128)(2,1)} copy(bf16[2048,1,2,128]{3,0,2,1:T(8,128)(2,1)S(1)} %maximum_bitcast_fusion) | data formatting | bytes 2097152 | tf_op jit(solution)/shard_map/reshape | solution.py:151
  313.2 7.2 %all-to-all-start.7 = ((bf16[2048,1,2,128]{3,2,1,0:T(2,128)(2,1)}), bf16[2048,1,2,128]{3,2,1,0:T(2,128)(2,1)S(1)}, u32[]{:S(2)}, u32[]{:S(2)}) async-start(bf16[2048,1,2,128]{3,2,1,0:T(2,128)(2,1)} %copy.183), calls=%async_computation.7 | async-start | bytes 2097152 | tf_op jit(solution)/shard_map/all_to_all | solution.py:152
  322.4 15.2 %all-to-all-done.7 = bf16[2048,1,2,128]{3,2,1,0:T(2,128)(2,1)S(1)} async-done(((bf16[2048,1,2,128]{3,2,1,0:T(2,128)(2,1)}), bf16[2048,1,2,128]{3,2,1,0:T(2,128)(2,1)S(1)}, u32[]{:S(2)}, u32[]{:S(2)}) %all-to-all-start.7) | async-done | bytes 1048608 | tf_op jit(solution)/shard_map/all_to_all | solution.py:152
  338.4 1.6 reshape.615
  (154 shorter events, 47.5 us)
Async XLA Ops:
  0.6 11.8 %copy-start.17 = (bf16[128,4096]{1,0:T(8,128)(2,1)S(1)}, bf16[128,4096]{1,0:T(8,128)(2,1)}, u32[]{:S(2)}) copy-start(bf16[128,4096]{1,0:T(8,128)(2,1)} %param.12) | copy-start | bytes 3145732
  3.0 26.7 %all-to-all-start.2 = ((bf16[128,16,256]{0,2,1:T(8,128)(2,1)}), bf16[128,16,256]{0,2,1:T(8,128)(2,1)S(1)}, u32[]{:S(2)}, u32[]{:S(2)}) async-start(bf16[128,16,256]{0,2,1:T(8,128)(2,1)} %bitcast.13), calls=%async_computation.2 | async-start | bytes 2097152 | tf_op jit(solution)/shard_map/all_to_all | solution.py:165
  12.5 21.6 %copy-start.18 = (bf16[128,4096]{1,0:T(8,128)(2,1)S(1)}, bf16[128,4096]{1,0:T(8,128)(2,1)}, u32[]{:S(2)}) copy-start(bf16[128,4096]{1,0:T(8,128)(2,1)} %param.11) | copy-start | bytes 3145732
  29.7 21.6 %all-to-all-start.1 = ((bf16[128,16,256]{0,2,1:T(8,128)(2,1)}), bf16[128,16,256]{0,2,1:T(8,128)(2,1)S(1)}, u32[]{:S(2)}, u32[]{:S(2)}) async-start(bf16[128,16,256]{0,2,1:T(8,128)(2,1)} %bitcast.7), calls=%async_computation.1 | async-start | bytes 2097152 | tf_op jit(solution)/shard_map/all_to_all | solution.py:164
  51.3 1.0 copy-start.10
  52.3 21.7 %all-to-all-start = ((bf16[128,16,256]{0,2,1:T(8,128)(2,1)}), bf16[128,16,256]{0,2,1:T(8,128)(2,1)S(1)}, u32[]{:S(2)}, u32[]{:S(2)}) async-start(bf16[128,16,256]{0,2,1:T(8,128)(2,1)} %bitcast.1), calls=%async_computation | async-start | bytes 2097152 | tf_op jit(solution)/shard_map/all_to_all | solution.py:163
  58.3 21.1 %copy-start.25 = (f32[256,16]{0,1:T(8,128)S(1)}, f32[256,16]{0,1:T(8,128)}, u32[]{:S(2)}) copy-start(f32[256,16]{0,1:T(8,128)} %param.15) | copy-start | bytes 49156
  58.3 21.1 %copy-start.26 = (f32[256,16]{0,1:T(8,128)S(1)}, f32[256,16]{0,1:T(8,128)}, u32[]{:S(2)}) copy-start(f32[256,16]{0,1:T(8,128)} %param.16) | copy-start | bytes 49156
  73.9 1.0 copy-start.8
  74.9 21.6 %all-to-all-start.6 = ((bf16[128,16,2,128]{3,0,2,1:T(8,128)(2,1)}), bf16[128,16,2,128]{3,0,2,1:T(8,128)(2,1)S(1)}, u32[]{:S(2)}, u32[]{:S(2)}) async-start(bf16[128,16,2,128]{3,0,2,1:T(8,128)(2,1)} %copy.171), calls=%async_computation.6 | async-start | bytes 2097152 | tf_op jit(solution)/shard_map/all_to_all | solution.py:187
  96.6 5.9 %copy-start.2 = (bf16[128,16,2,128]{3,0,2,1:T(8,128)(2,1)}, bf16[128,16,2,128]{3,0,2,1:T(8,128)(2,1)S(1)}, u32[]{:S(2)}) copy-start(bf16[128,16,2,128]{3,0,2,1:T(8,128)(2,1)S(1)} %all-to-all-done.6) | copy-start | bytes 3145732
  96.6 21.6 %all-to-all-start.5 = ((bf16[128,16,2,128]{3,0,2,1:T(8,128)(2,1)}), bf16[128,16,2,128]{3,0,2,1:T(8,128)(2,1)S(1)}, u32[]{:S(2)}, u32[]{:S(2)}) async-start(bf16[128,16,2,128]{3,0,2,1:T(8,128)(2,1)} %copy.168), calls=%async_computation.5 | async-start | bytes 2097152 | tf_op jit(solution)/shard_map/all_to_all | solution.py:186
  102.5 3.0 copy-start.11
  118.2 6.0 %copy-start.4 = (bf16[128,16,2,128]{3,0,2,1:T(8,128)(2,1)}, bf16[128,16,2,128]{3,0,2,1:T(8,128)(2,1)S(1)}, u32[]{:S(2)}) copy-start(bf16[128,16,2,128]{3,0,2,1:T(8,128)(2,1)S(1)} %all-to-all-done.5) | copy-start | bytes 3145732
  118.2 156.9 %all-to-all-start.4 = ((bf16[128,16,2,128]{3,0,2,1:T(8,128)(2,1)}), bf16[128,16,2,128]{3,0,2,1:T(8,128)(2,1)}, u32[]{:S(2)}, u32[]{:S(2)}) async-start(bf16[128,16,2,128]{3,0,2,1:T(8,128)(2,1)} %copy.165), calls=%async_computation.4 | async-start | bytes 2097152 | tf_op jit(solution)/shard_map/all_to_all | solution.py:185
  133.9 2.3 copy-start.30
  169.2 2.4 copy-start
  175.1 3.9 %copy-start.1 = (f32[64,128,64]{1,2,0:T(8,128)S(1)}, f32[64,128,64]{1,2,0:T(8,128)}, u32[]{:S(2)}) copy-start(f32[64,128,64]{1,2,0:T(8,128)} %fusion.397) | copy-start | bytes 6291460 | tf_op jit(solution)/shard_map/while
  184.8 3.0 copy-start.21
  187.9 1.0 copy-start.22
  198.3 2.3 copy-start.30
  233.6 2.4 copy-start
  239.5 3.9 %copy-start.1 = (f32[64,128,64]{1,2,0:T(8,128)S(1)}, f32[64,128,64]{1,2,0:T(8,128)}, u32[]{:S(2)}) copy-start(f32[64,128,64]{1,2,0:T(8,128)} %fusion.397) | copy-start | bytes 6291460 | tf_op jit(solution)/shard_map/while
  249.2 3.0 copy-start.21
  252.3 1.0 copy-start.22
  260.4 2.5 copy-start.5
  260.4 3.4 %copy-start.3 = (bf16[128,16,2,128]{3,0,2,1:T(8,128)(2,1)S(1)}, bf16[128,16,2,128]{3,0,2,1:T(8,128)(2,1)}, u32[]{:S(2)}) copy-start(bf16[128,16,2,128]{3,0,2,1:T(8,128)(2,1)} %copy-done.2) | copy-start | bytes 3145732
  264.9 2.4 copy-start.23
  265.7 2.9 copy-start.9
  270.2 1.9 copy-start.27
  270.2 1.9 copy-start.28
  270.2 2.0 copy-start.29
  275.1 38.1 %all-to-all-start.3 = ((bf16[16,128,256]{2,1,0:T(8,128)(2,1)}), bf16[16,128,256]{2,1,0:T(8,128)(2,1)S(1)}, u32[]{:S(2)}, u32[]{:S(2)}) async-start(bf16[16,128,256]{2,1,0:T(8,128)(2,1)} %bitcast.364), calls=%async_computation.3 | async-start | bytes 2097152 | tf_op jit(solution)/shard_map/all_to_all | solution.py:178
  282.3 1.4 copy-start.13
  282.4 1.6 copy-start.16
  283.7 1.1 copy-start.15
  283.8 1.1 copy-start.24
  283.9 1.3 copy-start.12
  283.9 1.6 copy-start.20
  287.5 2.5 copy-start.19
  289.9 2.6 copy-start.6
  294.0 2.1 copy-start.7
  298.3 1.1 copy-start.14
  313.2 24.4 %all-to-all-start.7 = ((bf16[2048,1,2,128]{3,2,1,0:T(2,128)(2,1)}), bf16[2048,1,2,128]{3,2,1,0:T(2,128)(2,1)S(1)}, u32[]{:S(2)}, u32[]{:S(2)}) async-start(bf16[2048,1,2,128]{3,2,1,0:T(2,128)(2,1)} %copy.183), calls=%async_computation.7 | async-start | bytes 2097152 | tf_op jit(solution)/shard_map/all_to_all | solution.py:152
where the time goes:
time: 347 us; the launch traced here: 340 us
  matrix products  135 us (39%)
  waiting for transfers between devices  67.6 us (19%)
  local copies, waits for them, and re-layouts  55.1 us (16%)
  starting transfers between devices  47.3 us (14%)
  other arithmetic  25.6 us (7%)
  loops' own time  8.2 us (2%)
    dot_general x4, matrix products, forward_dft(): part_im = -jnp.einsum('kn,nmc->kmc', sin_one, signal, precision=HIGHEST)  19.5 us
    all_to_all x1, waiting for transfers between devices, local(): lax.all_to_all(hyena_k, 'ctx', split_axis=1, concat_axis=0, tiled=True)  16 us
    all_to_all x1, waiting for transfers between devices, local(): lax.all_to_all(hyena_v, 'ctx', split_axis=1, concat_axis=0, tiled=True)  15.9 us
    all_to_all x1, waiting for transfers between devices, attend(): lax.all_to_all(attended, 'ctx', split_axis=0, concat_axis=1, tiled=True)  15.2 us
    dot_general x4, matrix products, forward_dft(): jnp.einsum('kmc,mj->kjc', turned_re, sin_two, precision=HIGHEST)  14.9 us
    unnamed x59, local copies, waits for them, and re-layouts  14.6 us
    dot_general x4, matrix products, forward_dft(): jnp.einsum('kmc,mj->kjc', turned_im, sin_two, precision=HIGHEST)  14.2 us
    dot_general x4, matrix products, forward_dft(): jnp.einsum('kmc,mj->kjc', turned_re, cos_two, precision=HIGHEST)  13.2 us
  transfers between devices with their start and end apart: 8, of which 6 were waited for; matrix products, arithmetic and copies ran while one was open for 60% of the time, Pallas kernels for 0%

commit v1 on v0

v1 whole, which is shorter than its diff:
```python
import functools
import math

import jax
import jax.numpy as jnp
from jax import lax
from jax.experimental import pallas as pl
from jax.experimental.pallas import tpu as pltpu
from jax.sharding import PartitionSpec as P

MESH = pl.DeviceIdType.MESH
f32, bf16 = jnp.float32, jnp.bfloat16

N = 16
ROWS = 128
SEQ = N * ROWS
D = 4096
MODES = 16
HEAD = 128
HEADS = D // HEAD // N
QBLOCK = 256
EXP2_SCALE = HEAD**-0.5 * math.log2(math.e)
STATE = MODES * 2


def row_of(j):
    return j % 2 * 16 + j // 2


def total(terms):
    while len(terms) > 1:
        terms = [a + b for a, b in zip(terms[::2], terms[1::2])]
    return terms[0]


def attend(q_ref, k_ref, v_ref, o_ref, block):
    end = (block + 1) * QBLOCK
    start = end - QBLOCK
    scores = lax.dot_general(
        q_ref[start:end, :], k_ref[:end, :], (((1,), (1,)), ((), ())), preferred_element_type=f32
    )
    row = lax.broadcasted_iota(jnp.int32, (QBLOCK, QBLOCK), 0)
    col = lax.broadcasted_iota(jnp.int32, (QBLOCK, QBLOCK), 1)
    diagonal = jnp.where(col <= row, scores[:, start:], -jnp.inf)
    top = jnp.max(diagonal, axis=1, keepdims=True)
    if block:
        top = jnp.maximum(top, jnp.max(scores[:, :start], axis=1, keepdims=True))
        scores = jnp.concatenate([scores[:, :start], diagonal], axis=1)
    else:
        scores = diagonal
    expo = jnp.exp2((scores - top) * EXP2_SCALE)
    denominator = jnp.sum(expo, axis=1, keepdims=True)
    mixed = jnp.dot(expo.astype(bf16), v_ref[:end, :], preferred_element_type=f32)
    o_ref[start:end, :] = (mixed / denominator).astype(bf16)


def short_filters(hx, halo, taps, qs, product, shifted):
    def column(j, carry):
        cs = pl.ds(pl.multiple_of(j * 128, 128), 128)

        def mix(f):
            x = hx[f, :, cs].astype(f32)
            shifted[f, 8 : 8 + ROWS, :] = x
            shifted[f, 6:8, :] = halo[2 * f : 2 * f + 2, cs]
            w = taps[f, :, cs]
            return (
                w[0:1] * x + w[1:2] * shifted[f, 7 : 7 + ROWS, :] + w[2:3] * shifted[f, 6 : 6 + ROWS, :]
            )

        qs[:, cs] = mix(0)
        both = (mix(1) * mix(2)).astype(bf16).astype(f32)
        product[pl.ds(row_of(j), ROWS, stride=32), :] = both
        return carry

    lax.fori_loop(0, D // 128, column, 0)


def mode_rows(ref, g, n, per_owner, first=0):
    return pl.ds(g % 2 * 8 * per_owner + first + n * 2 + g // 2, 8, stride=per_owner)


def scan(params, product, smooth, states):
    for g in range(4):
        power = [params[mode_rows(params, g, n, 2 * STATE), :] for n in range(MODES)]
        weight = [params[mode_rows(params, g, n, 2 * STATE, STATE), :] for n in range(MODES)]

        def step(t, state):
            rows = pl.ds(pl.multiple_of(t * 32 + g * 8, 8), 8)
            x = product[rows, :]
            state = [h * p + x for h, p in zip(state, power)]
            smooth[rows, :] = total([h * w for h, w in zip(state, weight)])
            return state

        state = lax.fori_loop(0, ROWS, step, [jnp.zeros((8, 128), f32)] * MODES, unroll=4)
        for n in range(MODES):
            states[mode_rows(states, g, n, STATE), :] = state[n]


def add_carried(params, carried, smooth):
    for g in range(4):
        power = [params[mode_rows(params, g, n, 2 * STATE), :] for n in range(MODES)]
        first = [
            params[mode_rows(params, g, n, 2 * STATE, STATE), :]
            * power[n]
            * carried[mode_rows(carried, g, n, STATE), :]
            for n in range(MODES)
        ]

        def step(t, term):
            rows = pl.ds(pl.multiple_of(t * 32 + g * 8, 8), 8)
            smooth[rows, :] = smooth[rows, :] + total(term)
            return [a * p for a, p in zip(term, power)]

        lax.fori_loop(0, ROWS, step, first, unroll=4)


def gate(smooth, qs, out):
    def column(j, carry):
        cs = pl.ds(pl.multiple_of(j * 128, 128), 128)
        y = smooth[pl.ds(row_of(j), ROWS, stride=32), :]
        out[:, cs] = (qs[:, cs] * y.astype(bf16).astype(f32)).astype(bf16)
        return carry

    lax.fori_loop(0, D // 128, column, 0, unroll=4)


def kernel(
    hq, hk, hv, taps_in, residue_in, decay_in, aq, ak, av,
    hyena_out, att_out,
    hx, taps, residue, decay, edge, halo, mine, params, leap, qs, product, smooth, shifted,
    ends, gathered, chained, carried, qkv, mixed, gated,
    load_sem, own_sem, out_sem,
    halo_s, halo_r, par_s, par_r, end_s, end_r, cha_s, cha_r, qkv_s, qkv_r, mix_s, mix_r,
):
    me = lax.axis_index("ctx")

    def moved(d, sign):
        z = (me // 2 + sign * (d // 2 % 4) + 4) % 4
        return (me // 8 + d // 8) % 2 * 8 + z * 2 + (me + d) % 2

    def target(d):
        return moved(d, 1)

    def source(d):
        return moved(d, -1)

    def each_peer(do):
        def step(d, carry):
            do(d)
            return carry

        lax.fori_loop(1, N, step, 0)

    def rows(p, count):
        return pl.ds(pl.multiple_of(p * count, count), count)

    def columns(p, h):
        return pl.ds(pl.multiple_of((p * HEADS + h) * HEAD, HEAD), HEAD)

    def remote(src, dst, send, recv, device):
        return pltpu.make_async_remote_copy(
            src_ref=src, dst_ref=dst, send_sem=send, recv_sem=recv,
            device_id={"ctx": device}, device_id_type=MESH,
        )

    loads = [
        pltpu.make_async_copy(src, dst, load_sem.at[i])
        for i, (src, dst) in enumerate(
            [(residue_in, residue), (decay_in, decay), (taps_in, taps)]
            + [(x, hx.at[f]) for f, x in enumerate((hq, hk, hv))]
        )
    ]
    for copy in loads:
        copy.start()

    barrier = pltpu.get_barrier_semaphore()
    each_peer(
        lambda d: pl.semaphore_signal(barrier, inc=1, device_id={"ctx": target(d)}, device_id_type=MESH)
    )

    att = (aq, ak, av)
    own = [
        [pltpu.make_async_copy(att[t].at[:, columns(me, h)], qkv.at[h, t, rows(me, ROWS)], own_sem.at[h, t]) for t in range(3)]
        for h in range(HEADS)
    ]
    for h in range(HEADS):
        for copy in own[h]:
            copy.start()

    loads[0].wait()
    loads[1].wait()
    rate = decay[...]
    weight = residue[...]
    for half in range(2):
        cs = slice(half * 128, half * 128 + 128)
        mine[pl.ds(half, MODES, stride=2), :] = jnp.exp(-rate[:, cs])
        mine[pl.ds(STATE + half, MODES, stride=2), :] = weight[:, cs]
        leap[pl.ds(half, MODES, stride=2), :] = jnp.exp(-(rate[:, cs] * float(ROWS)))
    params[rows(me, 2 * STATE), :] = mine[...]
    for copy in loads[2:]:
        copy.wait()
    edge[...] = jnp.zeros_like(edge)
    for f in range(3):
        edge[2 * f : 2 * f + 2, :] = hx[f, ROWS - 16 : ROWS, :].astype(f32)[14:16]

    pl.semaphore_wait(barrier, N - 1)

    halo_copy = remote(edge, halo, halo_s, halo_r, (me + 1) % N)
    halo_copy.start()

    def par_copy(d, p):
        return remote(mine, params.at[rows(p, 2 * STATE)], par_s.at[d], par_r.at[d], target(d))

    def qkv_copy(h, t, d, p):
        return remote(
            att[t].at[:, columns(target(d), h)], qkv.at[h, t, rows(p, ROWS)],
            qkv_s.at[h, t, d], qkv_r.at[h, t, d], target(d),
        )

    def end_copy(d, p):
        return remote(ends.at[rows(target(d), STATE)], gathered.at[rows(p, STATE)], end_s.at[d], end_r.at[d], target(d))

    def cha_copy(d, p):
        return remote(chained.at[rows(target(d), STATE)], carried.at[rows(p, STATE)], cha_s.at[d], cha_r.at[d], target(d))

    def mix_copy(h, d, p):
        return remote(
            mixed.at[h, rows(target(d), ROWS)], att_out.at[:, columns(p, h)],
            mix_s.at[h, d], mix_r.at[h, d], target(d),
        )

    def qkv_start(h):
        def one(d):
            for t in range(3):
                qkv_copy(h, t, d, me).start()

        each_peer(one)

    def qkv_wait(h):
        def one(d):
            for t in range(3):
                qkv_copy(h, t, d, source(d)).wait_recv()

        each_peer(one)
        for copy in own[h]:
            copy.wait()

    each_peer(lambda d: par_copy(d, me).start())
    qkv_start(0)

    halo_copy.wait_recv()

    @pl.when(me == 0)
    def _():
        halo[...] = jnp.zeros_like(halo)

    short_filters(hx, halo, taps, qs, product, shifted)
    each_peer(lambda d: par_copy(d, source(d)).wait_recv())
    scan(params, product, smooth, ends)
    gathered[rows(me, STATE), :] = ends[rows(me, STATE), :]
    each_peer(lambda d: end_copy(d, me).start())
    qkv_start(1)

    def attention(h):
        qkv_wait(h)
        for block in range(SEQ // QBLOCK):
            attend(qkv.at[h, 0], qkv.at[h, 1], qkv.at[h, 2], mixed.at[h], block)
        each_peer(lambda d: mix_copy(h, d, me).start())
        copy = pltpu.make_async_copy(mixed.at[h, rows(me, ROWS)], att_out.at[:, columns(me, h)], out_sem.at[h])
        copy.start()
        return copy

    kept = [attention(0)]

    each_peer(lambda d: end_copy(d, source(d)).wait_recv())

    def chain(p, state):
        chained[rows(p, STATE), :] = state
        return state * leap[...] + gathered[rows(p, STATE), :]

    lax.fori_loop(0, N, chain, jnp.zeros((STATE, 128), f32))
    carried[rows(me, STATE), :] = chained[rows(me, STATE), :]
    each_peer(lambda d: cha_copy(d, me).start())

    kept.append(attention(1))

    each_peer(lambda d: cha_copy(d, source(d)).wait_recv())
    add_carried(params, carried, smooth)
    gate(smooth, qs, gated)
    last = pltpu.make_async_copy(gated, hyena_out, out_sem.at[2])
    last.start()

    halo_copy.wait_send()

    def finish(d):
        par_copy(d, me).wait_send()
        end_copy(d, me).wait_send()
        cha_copy(d, me).wait_send()
        for h in range(HEADS):
            for t in range(3):
                qkv_copy(h, t, d, me).wait_send()
            mix_copy(h, d, me).wait_send()
            mix_copy(h, d, source(d)).wait_recv()

    each_peer(finish)
    for copy in kept:
        copy.wait()
    last.wait()


def local(hyena_q, hyena_k, hyena_v, short_filter, residue, decay_rate, att_query, att_key, att_value):
    residue, decay_rate = residue.T, decay_rate.T
    vmem = pltpu.VMEM
    dma = pltpu.SemaphoreType.DMA
    return pl.pallas_call(
        kernel,
        out_shape=(jax.ShapeDtypeStruct((ROWS, D), bf16), jax.ShapeDtypeStruct((ROWS, D), bf16)),
        in_specs=[pl.BlockSpec(memory_space=pltpu.HBM)] * 9,
        out_specs=(pl.BlockSpec(memory_space=pl.ANY), pl.BlockSpec(memory_space=pl.ANY)),
        scratch_shapes=[
            vmem((3, ROWS, D), bf16),
            vmem(short_filter.shape, f32),
            vmem(residue.shape, f32),
            vmem(decay_rate.shape, f32),
            vmem((8, D), f32),
            vmem((8, D), f32),
            vmem((2 * STATE, 128), f32),
            vmem((N * 2 * STATE, 128), f32),
            vmem((STATE, 128), f32),
            vmem((ROWS, D), f32),
            vmem((ROWS * 32, 128), f32),
            vmem((ROWS * 32, 128), f32),
            vmem((3, ROWS + 8, 128), f32),
            vmem((N * STATE, 128), f32),
            vmem((N * STATE, 128), f32),
            vmem((N * STATE, 128), f32),
            vmem((N * STATE, 128), f32),
            vmem((HEADS, 3, SEQ, HEAD), bf16),
            vmem((HEADS, SEQ, HEAD), bf16),
            vmem((ROWS, D), bf16),
            dma((6,)),
            dma((HEADS, 3)),
            dma((3,)),
            dma,
            dma,
            dma((N,)),
            dma((N,)),
            dma((N,)),
            dma((N,)),
            dma((N,)),
            dma((N,)),
            dma((HEADS, 3, N)),
            dma((HEADS, 3, N)),
            dma((HEADS, N)),
            dma((HEADS, N)),
        ],
        compiler_params=pltpu.CompilerParams(
            collective_id=0, has_side_effects=True, vmem_limit_bytes=63 * 2**20
        ),
    )(hyena_q, hyena_k, hyena_v, short_filter, residue, decay_rate, att_query, att_key, att_value)


def solution(mesh):
    rows = P(("dp", "ctx"), None)
    placed = (rows, rows, rows, P(), P("ctx", None), P("ctx", None), rows, rows, rows)
    return jax.shard_map(local, mesh=mesh, in_specs=placed, out_specs=(rows, rows), check_vma=False)
```

time: 347 us -> 78.1 us (0.23); the launches traced: 340 us -> 78 us
  matrix products: 135 us -> 0 us
  Pallas kernels: 0 us -> 74 us
  waiting for transfers between devices: 67.6 us -> 0 us
  local copies, waits for them, and re-layouts: 55.1 us -> 3.35 us
  starting transfers between devices: 47.3 us -> 0 us
  other arithmetic: 25.6 us -> 0 us
  loops' own time: 8.2 us -> 0 us
    dot_general x44 -> x0, matrix products: 135 us -> none  [the longest x4 19.5 us: forward_dft(): part_im = -jnp.einsum('kn,nmc->kmc', sin_one, signal, precision=HIGHEST)]
    pallas_call x0 -> x1, Pallas kernels: none -> 74 us  [local(): pl.pallas_call(kernel, out_shape=(jax.ShapeDtypeStruct((ROWS, D), bf16),...]
    all_to_all x8 -> x0, waiting for transfers between devices: 67.6 us -> none  [the longest x1 16 us: local(): lax.all_to_all(hyena_k, 'ctx', split_axis=1, concat_axis=0, tiled=True)]
    all_to_all x8 -> x0, starting transfers between devices: 47.3 us -> none  [the longest x1 9.46 us: local(): lax.all_to_all(hyena_v, 'ctx', split_axis=1, concat_axis=0, tiled=True)]
    reshape x7 -> x0, local copies, waits for them, and re-layouts: 15.1 us -> none  [the longest x1 9.47 us: attend(): jnp.concatenate(out_blocks, 0).reshape(length, 1, head_count, head_width)]
    convert_element_type x5 -> x0, other arithmetic: 13.9 us -> none  [the longest x1 6.23 us: local(): (key_mix * value_mix).astype(jnp.bfloat16)]
    unnamed x59 -> x4, local copies, waits for them, and re-layouts: 14.6 us -> 3.35 us
    another operation x1 -> x0, loops' own time: 8.2 us -> none  [long_conv(): results = lax.map(one_block, (blocks_in, residue_blocks, rate_blocks))]
  transfers between devices with their start and end apart: 8 -> 0, of which waited for: 6 -> 0; matrix products, arithmetic and copies ran while one was open for 60% -> 0% of each run, Pallas kernels for 0% -> 0%
where the time goes in v1:
time: 78.1 us; the launch traced here: 78 us
  Pallas kernels  74 us (95%)
  local copies, waits for them, and re-layouts  3.35 us (4%)
    pallas_call x1, Pallas kernels, local(): pl.pallas_call(kernel, out_shape=(jax.ShapeDtypeStruct((ROWS, D), bf16),...  74 us
    unnamed x4, local copies, waits for them, and re-layouts  3.35 us

profile of v1, /device:TPU:1, one launch (start us, length us, event | category | flops | bytes accessed | tf_op | source)
XLA Modules:
  0.0 78.0 jit_solution(5276913223429716400)
XLA Ops:
  0.6 74.0 %shard_map.104 = (bf16[128,4096]{1,0:T(8,128)(2,1)}, bf16[128,4096]{1,0:T(8,128)(2,1)}) custom-call(bf16[128,4096]{1,0:T(8,128)(2,1)} %hq.1, bf16[128,4096]{1,0:T(8,128)(2,1)} %hk.1, bf16[128,4096]{1,0:T(8,128)(2,1)} %hv.1, f32[3,3,4096]{2,1,0:T(4,128)} %taps_in.1, f32[16,256]{1,0:T(8,128)} %bitcast.2, f32[16,256]{1,0:T(8,128)} %bitcast.3, ...), custom_call_target="tpu_custom_call" | custom-call | tf_op jit(solution)/shard_map/pallas_call | solution.py:315
  74.6 0.0 copy-start
  74.6 2.4 %copy.13 = bf16[128,4096]{1,0:T(8,128)(2,1)} copy(bf16[128,4096]{1,0:T(8,128)(2,1)} %get-tuple-element.4) | data formatting | bytes 2097152
  77.0 0.0 copy-done
  77.0 1.0 %copy.14 = bf16[128,4096]{1,0:T(8,128)(2,1)} copy(bf16[128,4096]{1,0:T(8,128)(2,1)S(1)} %copy-done) | data formatting | bytes 2097152
Async XLA Ops:
  74.6 2.4 %copy-start = (bf16[128,4096]{1,0:T(8,128)(2,1)S(1)}, bf16[128,4096]{1,0:T(8,128)(2,1)}, u32[]{:S(2)}) copy-start(bf16[128,4096]{1,0:T(8,128)(2,1)} %get-tuple-element.5) | copy-start | bytes 3145732

commit v2 on v1

--- a/solution.py
+++ b/solution.py
@@ -12,6 +12,8 @@
 f32, bf16 = jnp.float32, jnp.bfloat16
 
 N = 16
+CHIPS = N // 2
+NEAR = CHIPS + 2
 ROWS = 128
 SEQ = N * ROWS
 D = 4096
@@ -24,7 +26,7 @@
 
 
 def row_of(j):
-    return j % 2 * 16 + j // 2
+    return j % 2 * 16 + j // 2 % 2 * 8 + j // 4
 
 
 def total(terms):
@@ -54,6 +56,22 @@
     o_ref[start:end, :] = (mixed / denominator).astype(bf16)
 
 
+def edge_at(j, f, r):
+    return pl.ds(j * 6 + 2 * f + r, 1)
+
+
+def pack_edge(hx, wide):
+    def column(j, carry):
+        cs = pl.ds(pl.multiple_of(j * 128, 128), 128)
+        for f in range(3):
+            last = hx[f, ROWS - 16 : ROWS, cs].astype(f32)
+            for r in range(2):
+                wide[edge_at(j, f, r), :] = last[14 + r : 15 + r]
+        return carry
+
+    lax.fori_loop(0, D // 128, column, 0)
+
+
 def short_filters(hx, halo, taps, qs, product, shifted):
     def column(j, carry):
         cs = pl.ds(pl.multiple_of(j * 128, 128), 128)
@@ -61,7 +79,8 @@
         def mix(f):
             x = hx[f, :, cs].astype(f32)
             shifted[f, 8 : 8 + ROWS, :] = x
-            shifted[f, 6:8, :] = halo[2 * f : 2 * f + 2, cs]
+            for r in range(2):
+                shifted[f, 6 + r : 7 + r, :] = halo[edge_at(j, f, r), :]
             w = taps[f, :, cs]
             return (
                 w[0:1] * x + w[1:2] * shifted[f, 7 : 7 + ROWS, :] + w[2:3] * shifted[f, 6 : 6 + ROWS, :]
@@ -127,12 +146,15 @@
 def kernel(
     hq, hk, hv, taps_in, residue_in, decay_in, aq, ak, av,
     hyena_out, att_out,
-    hx, taps, residue, decay, edge, halo, mine, params, leap, qs, product, smooth, shifted,
-    ends, gathered, chained, carried, qkv, mixed, gated,
-    load_sem, own_sem, out_sem,
-    halo_s, halo_r, par_s, par_r, end_s, end_r, cha_s, cha_r, qkv_s, qkv_r, mix_s, mix_r,
+    hx, taps, residue, decay, wide, edge, halo, mine, params, leap, step, qs, product, smooth, shifted,
+    ends, pair, joint, gathered, chained, start, beside, carried, qkv, mixed, gated,
+    ready, load_sem, own_sem, out_sem, one_s, one_r,
+    par_s, par_r, end_s, end_r, cha_s, cha_r, qkv_s, qkv_r, mix_s, mix_r,
 ):
     me = lax.axis_index("ctx")
+    core = me % 2
+    chip = me // 2
+    other = me + 1 - 2 * core
 
     def moved(d, sign):
         z = (me // 2 + sign * (d // 2 % 4) + 4) % 4
@@ -144,12 +166,19 @@
     def source(d):
         return moved(d, -1)
 
-    def each_peer(do):
-        def step(d, carry):
-            do(d)
+    def each_peer(do, last_first=False, begin=1, end=N):
+        def at(d, carry):
+            do(begin + end - 1 - d if last_first else d)
             return carry
 
-        lax.fori_loop(1, N, step, 0)
+        lax.fori_loop(begin, end, at, 0)
+
+    def each_chip(do, begin=1, end=CHIPS):
+        def at(e, carry):
+            do(2 * e)
+            return carry
+
+        lax.fori_loop(begin, end, at, 0)
 
     def rows(p, count):
         return pl.ds(pl.multiple_of(p * count, count), count)
@@ -170,17 +199,22 @@
             + [(x, hx.at[f]) for f, x in enumerate((hq, hk, hv))]
         )
     ]
+
+    barrier = pltpu.get_barrier_semaphore()
+    each_peer(
+        lambda d: pl.semaphore_signal(barrier, inc=1, device_id={"ctx": target(d)}, device_id_type=MESH),
+        last_first=True,
+        end=NEAR,
+    )
     for copy in loads:
         copy.start()
 
-    barrier = pltpu.get_barrier_semaphore()
-    each_peer(
-        lambda d: pl.semaphore_signal(barrier, inc=1, device_id={"ctx": target(d)}, device_id_type=MESH)
-    )
-
     att = (aq, ak, av)
     own = [
-        [pltpu.make_async_copy(att[t].at[:, columns(me, h)], qkv.at[h, t, rows(me, ROWS)], own_sem.at[h, t]) for t in range(3)]
+        [
+            pltpu.make_async_copy(att[t].at[:, columns(me, h)], qkv.at[h, t, rows(me, ROWS)], own_sem.at[h, t])
+            for t in range(3)
+        ]
         for h in range(HEADS)
     ]
     for h in range(HEADS):
@@ -195,21 +229,41 @@
         cs = slice(half * 128, half * 128 + 128)
         mine[pl.ds(half, MODES, stride=2), :] = jnp.exp(-rate[:, cs])
         mine[pl.ds(STATE + half, MODES, stride=2), :] = weight[:, cs]
-        leap[pl.ds(half, MODES, stride=2), :] = jnp.exp(-(rate[:, cs] * float(ROWS)))
-    params[rows(me, 2 * STATE), :] = mine[...]
+        leap[pl.ds(half, MODES, stride=2), :] = jnp.exp(-(rate[:, cs] * float(2 * ROWS)))
+    slot = core * CHIPS + chip
+    params[rows(slot, 2 * STATE), :] = mine[...]
     for copy in loads[2:]:
         copy.wait()
-    edge[...] = jnp.zeros_like(edge)
-    for f in range(3):
-        edge[2 * f : 2 * f + 2, :] = hx[f, ROWS - 16 : ROWS, :].astype(f32)[14:16]
-
-    pl.semaphore_wait(barrier, N - 1)
-
-    halo_copy = remote(edge, halo, halo_s, halo_r, (me + 1) % N)
-    halo_copy.start()
+    pack_edge(hx, wide)
+    edge[...] = wide[...].astype(bf16)
+
+    pl.semaphore_wait(barrier, NEAR - 1)
+    pl.semaphore_signal(ready, inc=1, device_id={"ctx": target(N // 2)}, device_id_type=MESH)
+
+    halo_copy = remote(edge, halo, one_s.at[0], one_r.at[0], (me + 1) % N)
+    half_rows = CHIPS * 2 * STATE
+    par_on = remote(
+        params.at[rows(core, half_rows)], params.at[rows(core, half_rows)], one_s.at[1], one_r.at[1], other
+    )
+    end_on = remote(ends.at[rows(1 - core, CHIPS * STATE)], pair, one_s.at[2], one_r.at[2], other)
+    cha_on = remote(beside, carried.at[rows(core, CHIPS * STATE)], one_s.at[3], one_r.at[3], other)
 
     def par_copy(d, p):
-        return remote(mine, params.at[rows(p, 2 * STATE)], par_s.at[d], par_r.at[d], target(d))
+        return remote(
+            mine, params.at[rows(core * CHIPS + p // 2, 2 * STATE)], par_s.at[d // 2], par_r.at[d // 2], target(d)
+        )
+
+    def end_copy(d, p):
+        return remote(
+            joint.at[rows(target(d) // 2, STATE)], gathered.at[rows(p // 2, STATE)],
+            end_s.at[d // 2], end_r.at[d // 2], target(d),
+        )
+
+    def cha_copy(d, p):
+        return remote(
+            chained.at[rows(target(d) // 2, STATE)], start.at[rows(p // 2, STATE)],
+            cha_s.at[d // 2], cha_r.at[d // 2], target(d),
+        )
 
     def qkv_copy(h, t, d, p):
         return remote(
@@ -217,24 +271,18 @@
             qkv_s.at[h, t, d], qkv_r.at[h, t, d], target(d),
         )
 
-    def end_copy(d, p):
-        return remote(ends.at[rows(target(d), STATE)], gathered.at[rows(p, STATE)], end_s.at[d], end_r.at[d], target(d))
-
-    def cha_copy(d, p):
-        return remote(chained.at[rows(target(d), STATE)], carried.at[rows(p, STATE)], cha_s.at[d], cha_r.at[d], target(d))
-
     def mix_copy(h, d, p):
         return remote(
             mixed.at[h, rows(target(d), ROWS)], att_out.at[:, columns(p, h)],
             mix_s.at[h, d], mix_r.at[h, d], target(d),
         )
 
-    def qkv_start(h):
+    def qkv_start(h, tensors, begin=1, end=N):
         def one(d):
-            for t in range(3):
+            for t in tensors:
                 qkv_copy(h, t, d, me).start()
 
-        each_peer(one)
+        each_peer(one, last_first=True, begin=begin, end=end)
 
     def qkv_wait(h):
         def one(d):
@@ -245,110 +293,185 @@
         for copy in own[h]:
             copy.wait()
 
-    each_peer(lambda d: par_copy(d, me).start())
-    qkv_start(0)
-
-    halo_copy.wait_recv()
+    each_chip(lambda d: par_copy(d, me).start(), 1, CHIPS // 2 + 1)
+    qkv_start(0, (0,), end=NEAR)
+    pl.semaphore_wait(ready, 1)
+    each_chip(lambda d: par_copy(d, me).start(), CHIPS // 2 + 1, CHIPS)
+
+    @pl.when(me < N - 1)
+    def _():
+        halo_copy.start()
+
+    qkv_start(0, (0,), begin=NEAR)
+    qkv_start(0, (1, 2))
+
+    @pl.when(me > 0)
+    def _():
+        halo_copy.wait_recv()
+        wide[...] = halo[...].astype(f32)
 
     @pl.when(me == 0)
     def _():
-        halo[...] = jnp.zeros_like(halo)
-
-    short_filters(hx, halo, taps, qs, product, shifted)
-    each_peer(lambda d: par_copy(d, source(d)).wait_recv())
+        wide[...] = jnp.zeros_like(wide)
+
+    short_filters(hx, wide, taps, qs, product, shifted)
+    each_chip(lambda d: par_copy(d, source(d)).wait_recv())
+    par_on.start()
+    par_on.wait_recv()
     scan(params, product, smooth, ends)
-    gathered[rows(me, STATE), :] = ends[rows(me, STATE), :]
-    each_peer(lambda d: end_copy(d, me).start())
-    qkv_start(1)
+    end_on.start()
+
+    for p in range(CHIPS):
+        power = params[pl.ds(pl.multiple_of(core * half_rows + p * 2 * STATE, STATE), STATE), :]
+        for _ in range(7):
+            power = power * power
+        step[p * STATE : (p + 1) * STATE, :] = power
+
+    end_on.wait_recv()
+    same = ends[rows(core, CHIPS * STATE), :]
+    first = jnp.where(core == 0, same, pair[...])
+    joint[...] = first * step[...] + jnp.where(core == 0, pair[...], same)
+    gathered[rows(chip, STATE), :] = joint[rows(chip, STATE), :]
+    each_chip(lambda d: end_copy(d, me).start())
+    qkv_start(1, (0, 1, 2))
 
     def attention(h):
         qkv_wait(h)
         for block in range(SEQ // QBLOCK):
             attend(qkv.at[h, 0], qkv.at[h, 1], qkv.at[h, 2], mixed.at[h], block)
-        each_peer(lambda d: mix_copy(h, d, me).start())
+
+    def mix_start(h):
+        each_peer(lambda d: mix_copy(h, d, me).start(), last_first=True)
         copy = pltpu.make_async_copy(mixed.at[h, rows(me, ROWS)], att_out.at[:, columns(me, h)], out_sem.at[h])
         copy.start()
         return copy
 
-    kept = [attention(0)]
-
-    each_peer(lambda d: end_copy(d, source(d)).wait_recv())
+    attention(0)
+
+    each_chip(lambda d: end_copy(d, source(d)).wait_recv())
 
     def chain(p, state):
         chained[rows(p, STATE), :] = state
         return state * leap[...] + gathered[rows(p, STATE), :]
 
-    lax.fori_loop(0, N, chain, jnp.zeros((STATE, 128), f32))
-    carried[rows(me, STATE), :] = chained[rows(me, STATE), :]
-    each_peer(lambda d: cha_copy(d, me).start())
-
-    kept.append(attention(1))
-
-    each_peer(lambda d: cha_copy(d, source(d)).wait_recv())
+    lax.fori_loop(0, CHIPS, chain, jnp.zeros((STATE, 128), f32))
+    start[rows(chip, STATE), :] = chained[rows(chip, STATE), :]
+    each_chip(lambda d: cha_copy(d, me).start())
+
+    kept = [mix_start(0)]
+
+    attention(1)
+    kept.append(mix_start(1))
+
+    each_chip(lambda d: cha_copy(d, source(d)).wait_recv())
+    same = ends[rows(core, CHIPS * STATE), :]
+    first = jnp.where(core == 0, same, pair[...])
+    even = start[...]
+    odd = even * step[...] + first
+    carried[rows(core, CHIPS * STATE), :] = jnp.where(core == 0, even, odd)
+    beside[...] = jnp.where(core == 0, odd, even)
+    cha_on.start()
+    cha_on.wait_recv()
     add_carried(params, carried, smooth)
     gate(smooth, qs, gated)
     last = pltpu.make_async_copy(gated, hyena_out, out_sem.at[2])
     last.start()
 
-    halo_copy.wait_send()
-
-    def finish(d):
+    @pl.when(me < N - 1)
+    def _():
+        halo_copy.wait_send()
+
+    for copy in (par_on, end_on, cha_on):
+        copy.wait_send()
+
+    def chips_done(d):
         par_copy(d, me).wait_send()
         end_copy(d, me).wait_send()
         cha_copy(d, me).wait_send()
+
+    def peers_done(d):
         for h in range(HEADS):
             for t in range(3):
                 qkv_copy(h, t, d, me).wait_send()
             mix_copy(h, d, me).wait_send()
             mix_copy(h, d, source(d)).wait_recv()
 
-    each_peer(finish)
+    each_chip(chips_done)
+    each_peer(peers_done)
     for copy in kept:
         copy.wait()
     last.wait()
+
+
+PIECES = 4
+
+
+def hand_over(a_in, b_in, a_out, b_out, room, sem):
+    reads, writes = [], []
+    for k, (src, dst) in enumerate(((a_in, a_out), (b_in, b_out))):
+        for i in range(PIECES):
+            piece = pl.ds(i * (ROWS // PIECES), ROWS // PIECES)
+            reads.append(pltpu.make_async_copy(src.at[piece], room.at[k, piece], sem.at[0, k, i]))
+            writes.append(pltpu.make_async_copy(room.at[k, piece], dst.at[piece], sem.at[1, k, i]))
+    for copy in reads:
+        copy.start()
+    for read, write in zip(reads, writes):
+        read.wait()
+        write.start()
+    for copy in writes:
+        copy.wait()
 
 
 def local(hyena_q, hyena_k, hyena_v, short_filter, residue, decay_rate, att_query, att_key, att_value):
     residue, decay_rate = residue.T, decay_rate.T
     vmem = pltpu.VMEM
     dma = pltpu.SemaphoreType.DMA
-    return pl.pallas_call(
+    hbm = pl.BlockSpec(memory_space=pltpu.HBM)
+    result = jax.ShapeDtypeStruct((ROWS, D), bf16)
+    hyena_out, att_out = pl.pallas_call(
         kernel,
-        out_shape=(jax.ShapeDtypeStruct((ROWS, D), bf16), jax.ShapeDtypeStruct((ROWS, D), bf16)),
-        in_specs=[pl.BlockSpec(memory_space=pltpu.HBM)] * 9,
-        out_specs=(pl.BlockSpec(memory_space=pl.ANY), pl.BlockSpec(memory_space=pl.ANY)),
+        out_shape=(result, result),
+        in_specs=[hbm] * 9,
+        out_specs=(hbm, hbm),
         scratch_shapes=[
             vmem((3, ROWS, D), bf16),
             vmem(short_filter.shape, f32),
             vmem(residue.shape, f32),
             vmem(decay_rate.shape, f32),
-            vmem((8, D), f32),
-            vmem((8, D), f32),
+            vmem((6 * D // 128, 128), f32),
+            vmem((6 * D // 128, 128), bf16),
+            vmem((6 * D // 128, 128), bf16),
             vmem((2 * STATE, 128), f32),
             vmem((N * 2 * STATE, 128), f32),
             vmem((STATE, 128), f32),
+            vmem((CHIPS * STATE, 128), f32),
             vmem((ROWS, D), f32),
             vmem((ROWS * 32, 128), f32),
             vmem((ROWS * 32, 128), f32),
             vmem((3, ROWS + 8, 128), f32),
             vmem((N * STATE, 128), f32),
-            vmem((N * STATE, 128), f32),
-            vmem((N * STATE, 128), f32),
+            vmem((CHIPS * STATE, 128), f32),
+            vmem((CHIPS * STATE, 128), f32),
+            vmem((CHIPS * STATE, 128), f32),
+            vmem((CHIPS * STATE, 128), f32),
+            vmem((CHIPS * STATE, 128), f32),
+            vmem((CHIPS * STATE, 128), f32),
             vmem((N * STATE, 128), f32),
             vmem((HEADS, 3, SEQ, HEAD), bf16),
             vmem((HEADS, SEQ, HEAD), bf16),
             vmem((ROWS, D), bf16),
+            pltpu.SemaphoreType.REGULAR,
             dma((6,)),
             dma((HEADS, 3)),
             dma((3,)),
-            dma,
-            dma,
-            dma((N,)),
-            dma((N,)),
-            dma((N,)),
-            dma((N,)),
-            dma((N,)),
-            dma((N,)),
+            dma((4,)),
+            dma((4,)),
+            dma((CHIPS,)),
+            dma((CHIPS,)),
+            dma((CHIPS,)),
+            dma((CHIPS,)),
+            dma((CHIPS,)),
+            dma((CHIPS,)),
             dma((HEADS, 3, N)),
             dma((HEADS, 3, N)),
             dma((HEADS, N)),
@@ -358,6 +481,14 @@
             collective_id=0, has_side_effects=True, vmem_limit_bytes=63 * 2**20
         ),
     )(hyena_q, hyena_k, hyena_v, short_filter, residue, decay_rate, att_query, att_key, att_value)
+    return pl.pallas_call(
+        hand_over,
+        out_shape=(result, result),
+        in_specs=[hbm, hbm],
+        out_specs=(hbm, hbm),
+        scratch_shapes=[vmem((2, ROWS, D), bf16), dma((2, 2, PIECES))],
+        compiler_params=pltpu.CompilerParams(vmem_limit_bytes=63 * 2**20),
+    )(hyena_out, att_out)
 
 
 def solution(mesh):

time: 78.1 us -> 68.4 us (0.88)
  Pallas kernels: 74 us -> 67.6 us
  local copies, waits for them, and re-layouts: 3.35 us -> 0 us
    pallas_call x1 -> x2, Pallas kernels: 74 us -> 67.6 us  [the longest x1 65.2 us: local(): pl.pallas_call(kernel, out_shape=(result, result), in_specs=[hbm] * 9, ou...]
    unnamed x4 -> x0, local copies, waits for them, and re-layouts: 3.35 us -> none
where the time goes in v2:
time: 68.4 us; the launch traced here: 68.2 us
  Pallas kernels  67.6 us (99%)
    pallas_call x1, Pallas kernels, local(): pl.pallas_call(kernel, out_shape=(result, result), in_specs=[hbm] * 9, ou...  65.2 us
    pallas_call x1, Pallas kernels, local(): pl.pallas_call(hand_over, out_shape=(result, result), in_specs=[hbm, hbm]...  2.4 us

profile of v2, /device:TPU:1, one launch (start us, length us, event | category | flops | bytes accessed | tf_op | source)
XLA Modules:
  0.0 68.2 jit_solution(6774727310642084891)
XLA Ops:
  0.6 65.2 %shard_map.104 = (bf16[128,4096]{1,0:T(8,128)(2,1)}, bf16[128,4096]{1,0:T(8,128)(2,1)}) custom-call(bf16[128,4096]{1,0:T(8,128)(2,1)} %hq.1, bf16[128,4096]{1,0:T(8,128)(2,1)} %hk.1, bf16[128,4096]{1,0:T(8,128)(2,1)} %hv.1, f32[3,3,4096]{2,1,0:T(4,128)} %taps_in.1, f32[16,256]{1,0:T(8,128)} %bitcast.2, f32[16,256]{1,0:T(8,128)} %bitcast.3, ...), custom_call_target="tpu_custom_call" | custom-call | tf_op jit(solution)/shard_map/pallas_call | solution.py:431
  65.8 2.4 %shard_map.105 = (bf16[128,4096]{1,0:T(8,128)(2,1)}, bf16[128,4096]{1,0:T(8,128)(2,1)}) custom-call(bf16[128,4096]{1,0:T(8,128)(2,1)} %get-tuple-element.4.a_in, bf16[128,4096]{1,0:T(8,128)(2,1)} %get-tuple-element.5.b_in), custom_call_target="tpu_custom_call" | custom-call | tf_op jit(solution)/shard_map/pallas_call | solution.py:484

commit v3 on v2

--- a/solution.py
+++ b/solution.py
@@ -148,7 +148,7 @@
     hyena_out, att_out,
     hx, taps, residue, decay, wide, edge, halo, mine, params, leap, step, qs, product, smooth, shifted,
     ends, pair, joint, gathered, chained, start, beside, carried, qkv, mixed, gated,
-    ready, load_sem, own_sem, out_sem, one_s, one_r,
+    ready, load_sem, out_sem, one_s, one_r,
     par_s, par_r, end_s, end_r, cha_s, cha_r, qkv_s, qkv_r, mix_s, mix_r,
 ):
     me = lax.axis_index("ctx")
@@ -156,15 +156,9 @@
     chip = me // 2
     other = me + 1 - 2 * core
 
-    def moved(d, sign):
-        z = (me // 2 + sign * (d // 2 % 4) + 4) % 4
+    def target(d):
+        z = (chip + d // 2) % 4
         return (me // 8 + d // 8) % 2 * 8 + z * 2 + (me + d) % 2
-
-    def target(d):
-        return moved(d, 1)
-
-    def source(d):
-        return moved(d, -1)
 
     def each_peer(do, last_first=False, begin=1, end=N):
         def at(d, carry):
@@ -193,12 +187,19 @@
         )
 
     loads = [
-        pltpu.make_async_copy(src, dst, load_sem.at[i])
+        pltpu.make_async_copy(src, dst, load_sem.at[min(i, 3)])
         for i, (src, dst) in enumerate(
             [(residue_in, residue), (decay_in, decay), (taps_in, taps)]
             + [(x, hx.at[f]) for f, x in enumerate((hq, hk, hv))]
         )
     ]
+
+    def all_in(ref, sem):
+        pltpu.make_async_copy(ref, ref, sem).wait()
+
+    def all_out(ref, sem):
+        remote(ref, ref, sem, sem, other).wait_send()
+
 
     barrier = pltpu.get_barrier_semaphore()
     each_peer(
@@ -210,16 +211,11 @@
         copy.start()
 
     att = (aq, ak, av)
-    own = [
-        [
-            pltpu.make_async_copy(att[t].at[:, columns(me, h)], qkv.at[h, t, rows(me, ROWS)], own_sem.at[h, t])
-            for t in range(3)
-        ]
-        for h in range(HEADS)
-    ]
     for h in range(HEADS):
-        for copy in own[h]:
-            copy.start()
+        for t in range(3):
+            pltpu.make_async_copy(
+                att[t].at[:, columns(me, h)], qkv.at[h, t, rows(me, ROWS)], qkv_r.at[h]
+            ).start()
 
     loads[0].wait()
     loads[1].wait()
@@ -232,8 +228,8 @@
         leap[pl.ds(half, MODES, stride=2), :] = jnp.exp(-(rate[:, cs] * float(2 * ROWS)))
     slot = core * CHIPS + chip
     params[rows(slot, 2 * STATE), :] = mine[...]
-    for copy in loads[2:]:
-        copy.wait()
+    loads[2].wait()
+    all_in(hx, load_sem.at[3])
     pack_edge(hx, wide)
     edge[...] = wide[...].astype(bf16)
 
@@ -250,31 +246,31 @@
 
     def par_copy(d, p):
         return remote(
-            mine, params.at[rows(core * CHIPS + p // 2, 2 * STATE)], par_s.at[d // 2], par_r.at[d // 2], target(d)
+            mine, params.at[rows(core * CHIPS + p // 2, 2 * STATE)], par_s, par_r, target(d)
         )
 
     def end_copy(d, p):
         return remote(
             joint.at[rows(target(d) // 2, STATE)], gathered.at[rows(p // 2, STATE)],
-            end_s.at[d // 2], end_r.at[d // 2], target(d),
+            end_s, end_r, target(d),
         )
 
     def cha_copy(d, p):
         return remote(
             chained.at[rows(target(d) // 2, STATE)], start.at[rows(p // 2, STATE)],
-            cha_s.at[d // 2], cha_r.at[d // 2], target(d),
+            cha_s, cha_r, target(d),
         )
 
     def qkv_copy(h, t, d, p):
         return remote(
             att[t].at[:, columns(target(d), h)], qkv.at[h, t, rows(p, ROWS)],
-            qkv_s.at[h, t, d], qkv_r.at[h, t, d], target(d),
+            qkv_s, qkv_r.at[h], target(d),
         )
 
     def mix_copy(h, d, p):
         return remote(
             mixed.at[h, rows(target(d), ROWS)], att_out.at[:, columns(p, h)],
-            mix_s.at[h, d], mix_r.at[h, d], target(d),
+            mix_s, mix_r, target(d),
         )
 
     def qkv_start(h, tensors, begin=1, end=N):
@@ -284,15 +280,6 @@
 
         each_peer(one, last_first=True, begin=begin, end=end)
 
-    def qkv_wait(h):
-        def one(d):
-            for t in range(3):
-                qkv_copy(h, t, d, source(d)).wait_recv()
-
-        each_peer(one)
-        for copy in own[h]:
-            copy.wait()
-
     each_chip(lambda d: par_copy(d, me).start(), 1, CHIPS // 2 + 1)
     qkv_start(0, (0,), end=NEAR)
     pl.semaphore_wait(ready, 1)
@@ -315,7 +302,7 @@
         wide[...] = jnp.zeros_like(wide)
 
     short_filters(hx, wide, taps, qs, product, shifted)
-    each_chip(lambda d: par_copy(d, source(d)).wait_recv())
+    all_in(params.at[pl.ds(0, (CHIPS - 1) * 2 * STATE)], par_r)
     par_on.start()
     par_on.wait_recv()
     scan(params, product, smooth, ends)
@@ -336,19 +323,17 @@
     qkv_start(1, (0, 1, 2))
 
     def attention(h):
-        qkv_wait(h)
+        all_in(qkv.at[h], qkv_r.at[h])
         for block in range(SEQ // QBLOCK):
             attend(qkv.at[h, 0], qkv.at[h, 1], qkv.at[h, 2], mixed.at[h], block)
 
     def mix_start(h):
         each_peer(lambda d: mix_copy(h, d, me).start(), last_first=True)
-        copy = pltpu.make_async_copy(mixed.at[h, rows(me, ROWS)], att_out.at[:, columns(me, h)], out_sem.at[h])
-        copy.start()
-        return copy
+        pltpu.make_async_copy(mixed.at[h, rows(me, ROWS)], att_out.at[:, columns(me, h)], mix_r).start()
 
     attention(0)
 
-    each_chip(lambda d: end_copy(d, source(d)).wait_recv())
+    all_in(gathered.at[pl.ds(0, (CHIPS - 1) * STATE)], end_r)
 
     def chain(p, state):
         chained[rows(p, STATE), :] = state
@@ -358,12 +343,12 @@
     start[rows(chip, STATE), :] = chained[rows(chip, STATE), :]
     each_chip(lambda d: cha_copy(d, me).start())
 
-    kept = [mix_start(0)]
+    mix_start(0)
 
     attention(1)
-    kept.append(mix_start(1))
-
-    each_chip(lambda d: cha_copy(d, source(d)).wait_recv())
+    mix_start(1)
+
+    all_in(start.at[pl.ds(0, (CHIPS - 1) * STATE)], cha_r)
     same = ends[rows(core, CHIPS * STATE), :]
     first = jnp.where(core == 0, same, pair[...])
     even = start[...]
@@ -374,7 +359,7 @@
     cha_on.wait_recv()
     add_carried(params, carried, smooth)
     gate(smooth, qs, gated)
-    last = pltpu.make_async_copy(gated, hyena_out, out_sem.at[2])
+    last = pltpu.make_async_copy(gated, hyena_out, out_sem)
     last.start()
 
     @pl.when(me < N - 1)
@@ -384,22 +369,12 @@
     for copy in (par_on, end_on, cha_on):
         copy.wait_send()
 
-    def chips_done(d):
-        par_copy(d, me).wait_send()
-        end_copy(d, me).wait_send()
-        cha_copy(d, me).wait_send()
-
-    def peers_done(d):
-        for h in range(HEADS):
-            for t in range(3):
-                qkv_copy(h, t, d, me).wait_send()
-            mix_copy(h, d, me).wait_send()
-            mix_copy(h, d, source(d)).wait_recv()
-
-    each_chip(chips_done)
-    each_peer(peers_done)
-    for copy in kept:
-        copy.wait()
+    all_out(params.at[pl.ds(0, (CHIPS - 1) * 2 * STATE)], par_s)
+    all_out(joint.at[pl.ds(0, (CHIPS - 1) * STATE)], end_s)
+    all_out(chained.at[pl.ds(0, (CHIPS - 1) * STATE)], cha_s)
+    all_out(qkv.at[:, :, pl.ds(0, (N - 1) * ROWS)], qkv_s)
+    all_out(mixed.at[:, pl.ds(0, (N - 1) * ROWS)], mix_s)
+    all_in(att_out, mix_r)
     last.wait()
 
 
@@ -461,21 +436,20 @@
             vmem((HEADS, SEQ, HEAD), bf16),
             vmem((ROWS, D), bf16),
             pltpu.SemaphoreType.REGULAR,
-            dma((6,)),
-            dma((HEADS, 3)),
-            dma((3,)),
+            dma((4,)),
+            dma,
             dma((4,)),
             dma((4,)),
-            dma((CHIPS,)),
-            dma((CHIPS,)),
-            dma((CHIPS,)),
-            dma((CHIPS,)),
-            dma((CHIPS,)),
-            dma((CHIPS,)),
-            dma((HEADS, 3, N)),
-            dma((HEADS, 3, N)),
-            dma((HEADS, N)),
-            dma((HEADS, N)),
+            dma,
+            dma,
+            dma,
+            dma,
+            dma,
+            dma,
+            dma,
+            dma((HEADS,)),
+            dma,
+            dma,
         ],
         compiler_params=pltpu.CompilerParams(
             collective_id=0, has_side_effects=True, vmem_limit_bytes=63 * 2**20

time: 68.4 us -> 65.4 us (0.956)
  Pallas kernels: 67.6 us -> 64.6 us
    pallas_call x1, Pallas kernels: 65.2 us -> 62.2 us  [local(): pl.pallas_call(kernel, out_shape=(result, result), in_specs=[hbm] * 9, ou...]
where the time goes in v3:
time: 65.4 us; the launch traced here: 65.3 us
  Pallas kernels  64.6 us (99%)
    pallas_call x1, Pallas kernels, local(): pl.pallas_call(kernel, out_shape=(result, result), in_specs=[hbm] * 9, ou...  62.2 us
    pallas_call x1, Pallas kernels, local(): pl.pallas_call(hand_over, out_shape=(result, result), in_specs=[hbm, hbm]...  2.4 us

profile of v3, /device:TPU:1, one launch (start us, length us, event | category | flops | bytes accessed | tf_op | source)
XLA Modules:
  0.0 65.3 jit_solution(1362442631252245828)
XLA Ops:
  0.6 62.2 %shard_map.104 = (bf16[128,4096]{1,0:T(8,128)(2,1)}, bf16[128,4096]{1,0:T(8,128)(2,1)}) custom-call(bf16[128,4096]{1,0:T(8,128)(2,1)} %hq.1, bf16[128,4096]{1,0:T(8,128)(2,1)} %hk.1, bf16[128,4096]{1,0:T(8,128)(2,1)} %hv.1, f32[3,3,4096]{2,1,0:T(4,128)} %taps_in.1, f32[16,256]{1,0:T(8,128)} %bitcast.2, f32[16,256]{1,0:T(8,128)} %bitcast.3, ...), custom_call_target="tpu_custom_call" | custom-call | tf_op jit(solution)/shard_map/pallas_call | solution.py:406
  62.9 2.4 %shard_map.105 = (bf16[128,4096]{1,0:T(8,128)(2,1)}, bf16[128,4096]{1,0:T(8,128)(2,1)}) custom-call(bf16[128,4096]{1,0:T(8,128)(2,1)} %get-tuple-element.4.a_in, bf16[128,4096]{1,0:T(8,128)(2,1)} %get-tuple-element.5.b_in), custom_call_target="tpu_custom_call" | custom-call | tf_op jit(solution)/shard_map/pallas_call | solution.py:458

commit v4 on v3

--- a/solution.py
+++ b/solution.py
@@ -35,7 +35,7 @@
     return terms[0]
 
 
-def attend(q_ref, k_ref, v_ref, o_ref, block):
+def weigh(q_ref, k_ref, weights, sums, block):
     end = (block + 1) * QBLOCK
     start = end - QBLOCK
     scores = lax.dot_general(
@@ -51,9 +51,15 @@
     else:
         scores = diagonal
     expo = jnp.exp2((scores - top) * EXP2_SCALE)
-    denominator = jnp.sum(expo, axis=1, keepdims=True)
-    mixed = jnp.dot(expo.astype(bf16), v_ref[:end, :], preferred_element_type=f32)
-    o_ref[start:end, :] = (mixed / denominator).astype(bf16)
+    sums[start:end, :] = jnp.broadcast_to(jnp.sum(expo, axis=1, keepdims=True), (QBLOCK, HEAD))
+    weights[start:end, :end] = expo.astype(bf16)
+
+
+def blend(weights, sums, v_ref, o_ref, block):
+    end = (block + 1) * QBLOCK
+    start = end - QBLOCK
+    mixed = jnp.dot(weights[start:end, :end], v_ref[:end, :], preferred_element_type=f32)
+    o_ref[start:end, :] = (mixed / sums[start:end, :]).astype(bf16)
 
 
 def edge_at(j, f, r):
@@ -147,7 +153,7 @@
     hq, hk, hv, taps_in, residue_in, decay_in, aq, ak, av,
     hyena_out, att_out,
     hx, taps, residue, decay, wide, edge, halo, mine, params, leap, step, qs, product, smooth, shifted,
-    ends, pair, joint, gathered, chained, start, beside, carried, qkv, mixed, gated,
+    ends, pair, joint, gathered, chained, start, beside, carried, qkv, weights, sums, mixed, gated,
     ready, load_sem, out_sem, one_s, one_r,
     par_s, par_r, end_s, end_r, cha_s, cha_r, qkv_s, qkv_r, mix_s, mix_r,
 ):
@@ -214,7 +220,7 @@
     for h in range(HEADS):
         for t in range(3):
             pltpu.make_async_copy(
-                att[t].at[:, columns(me, h)], qkv.at[h, t, rows(me, ROWS)], qkv_r.at[h]
+                att[t].at[:, columns(me, h)], qkv.at[h, t, rows(me, ROWS)], qkv_r.at[h, t // 2]
             ).start()
 
     loads[0].wait()
@@ -264,7 +270,7 @@
     def qkv_copy(h, t, d, p):
         return remote(
             att[t].at[:, columns(target(d), h)], qkv.at[h, t, rows(p, ROWS)],
-            qkv_s, qkv_r.at[h], target(d),
+            qkv_s, qkv_r.at[h, t // 2], target(d),
         )
 
     def mix_copy(h, d, p):
@@ -291,6 +297,7 @@
 
     qkv_start(0, (0,), begin=NEAR)
     qkv_start(0, (1, 2))
+    qkv_start(1, (0,))
 
     @pl.when(me > 0)
     def _():
@@ -320,12 +327,16 @@
     joint[...] = first * step[...] + jnp.where(core == 0, pair[...], same)
     gathered[rows(chip, STATE), :] = joint[rows(chip, STATE), :]
     each_chip(lambda d: end_copy(d, me).start())
-    qkv_start(1, (0, 1, 2))
+    qkv_start(1, (1,))
+    qkv_start(1, (2,))
 
     def attention(h):
-        all_in(qkv.at[h], qkv_r.at[h])
+        all_in(qkv.at[h, pl.ds(0, 2)], qkv_r.at[h, 0])
         for block in range(SEQ // QBLOCK):
-            attend(qkv.at[h, 0], qkv.at[h, 1], qkv.at[h, 2], mixed.at[h], block)
+            weigh(qkv.at[h, 0], qkv.at[h, 1], weights, sums, block)
+        all_in(qkv.at[h, 2], qkv_r.at[h, 1])
+        for block in range(SEQ // QBLOCK):
+            blend(weights, sums, qkv.at[h, 2], mixed.at[h], block)
 
     def mix_start(h):
         each_peer(lambda d: mix_copy(h, d, me).start(), last_first=True)
@@ -433,6 +444,8 @@
             vmem((CHIPS * STATE, 128), f32),
             vmem((N * STATE, 128), f32),
             vmem((HEADS, 3, SEQ, HEAD), bf16),
+            vmem((SEQ, SEQ), bf16),
+            vmem((SEQ, HEAD), f32),
             vmem((HEADS, SEQ, HEAD), bf16),
             vmem((ROWS, D), bf16),
             pltpu.SemaphoreType.REGULAR,
@@ -447,7 +460,7 @@
             dma,
             dma,
             dma,
-            dma((HEADS,)),
+            dma((HEADS, 2)),
             dma,
             dma,
         ],

time: 65.4 us -> 63.9 us (0.977)
  Pallas kernels: 64.6 us -> 63 us
    pallas_call x1, Pallas kernels: 62.2 us -> 60.6 us  [local(): pl.pallas_call(kernel, out_shape=(result, result), in_specs=[hbm] * 9, ou...]
where the time goes in v4:
time: 63.9 us; the launch traced here: 63.7 us
  Pallas kernels  63 us (99%)
  between operations  0.64 us (1%)
    pallas_call x1, Pallas kernels, local(): pl.pallas_call(kernel, out_shape=(result, result), in_specs=[hbm] * 9, ou...  60.6 us
    pallas_call x1, Pallas kernels, local(): pl.pallas_call(hand_over, out_shape=(result, result), in_specs=[hbm, hbm]...  2.4 us

profile of v4, /device:TPU:1, one launch (start us, length us, event | category | flops | bytes accessed | tf_op | source)
XLA Modules:
  0.0 63.7 jit_solution(4310030362052698631)
XLA Ops:
  0.6 60.6 %shard_map.104 = (bf16[128,4096]{1,0:T(8,128)(2,1)}, bf16[128,4096]{1,0:T(8,128)(2,1)}) custom-call(bf16[128,4096]{1,0:T(8,128)(2,1)} %hq.1, bf16[128,4096]{1,0:T(8,128)(2,1)} %hk.1, bf16[128,4096]{1,0:T(8,128)(2,1)} %hv.1, f32[3,3,4096]{2,1,0:T(4,128)} %taps_in.1, f32[16,256]{1,0:T(8,128)} %bitcast.2, f32[16,256]{1,0:T(8,128)} %bitcast.3, ...), custom_call_target="tpu_custom_call" | custom-call | tf_op jit(solution)/shard_map/pallas_call | solution.py:417
  61.3 2.4 %shard_map.105 = (bf16[128,4096]{1,0:T(8,128)(2,1)}, bf16[128,4096]{1,0:T(8,128)(2,1)}) custom-call(bf16[128,4096]{1,0:T(8,128)(2,1)} %get-tuple-element.4.a_in, bf16[128,4096]{1,0:T(8,128)(2,1)} %get-tuple-element.5.b_in), custom_call_target="tpu_custom_call" | custom-call | tf_op jit(solution)/shard_map/pallas_call | solution.py:471

commit v5 on v4

--- a/solution.py
+++ b/solution.py
@@ -22,6 +22,7 @@
 HEADS = D // HEAD // N
 QBLOCK = 256
 EXP2_SCALE = HEAD**-0.5 * math.log2(math.e)
+EDGE = 6 * D // 128
 STATE = MODES * 2
 
 
@@ -233,11 +234,11 @@
         mine[pl.ds(STATE + half, MODES, stride=2), :] = weight[:, cs]
         leap[pl.ds(half, MODES, stride=2), :] = jnp.exp(-(rate[:, cs] * float(2 * ROWS)))
     slot = core * CHIPS + chip
-    params[rows(slot, 2 * STATE), :] = mine[...]
+    params[rows(slot, 2 * STATE), :] = mine[: 2 * STATE, :]
     loads[2].wait()
     all_in(hx, load_sem.at[3])
     pack_edge(hx, wide)
-    edge[...] = wide[...].astype(bf16)
+    edge[...] = wide[:EDGE, :].astype(bf16)
 
     pl.semaphore_wait(barrier, NEAR - 1)
     pl.semaphore_signal(ready, inc=1, device_id={"ctx": target(N // 2)}, device_id_type=MESH)
@@ -252,7 +253,7 @@
 
     def par_copy(d, p):
         return remote(
-            mine, params.at[rows(core * CHIPS + p // 2, 2 * STATE)], par_s, par_r, target(d)
+            mine.at[pl.ds(0, 2 * STATE)], params.at[rows(core * CHIPS + p // 2, 2 * STATE)], par_s, par_r, target(d)
         )
 
     def end_copy(d, p):
@@ -302,7 +303,7 @@
     @pl.when(me > 0)
     def _():
         halo_copy.wait_recv()
-        wide[...] = halo[...].astype(f32)
+        wide[:EDGE, :] = halo[...].astype(f32)
 
     @pl.when(me == 0)
     def _():
@@ -348,7 +349,7 @@
 
     def chain(p, state):
         chained[rows(p, STATE), :] = state
-        return state * leap[...] + gathered[rows(p, STATE), :]
+        return state * leap[:STATE, :] + gathered[rows(p, STATE), :]
 
     lax.fori_loop(0, CHIPS, chain, jnp.zeros((STATE, 128), f32))
     start[rows(chip, STATE), :] = chained[rows(chip, STATE), :]
@@ -424,25 +425,25 @@
             vmem(short_filter.shape, f32),
             vmem(residue.shape, f32),
             vmem(decay_rate.shape, f32),
-            vmem((6 * D // 128, 128), f32),
-            vmem((6 * D // 128, 128), bf16),
-            vmem((6 * D // 128, 128), bf16),
-            vmem((2 * STATE, 128), f32),
-            vmem((N * 2 * STATE, 128), f32),
-            vmem((STATE, 128), f32),
+            vmem((EDGE + 8, 128), f32),
+            vmem((EDGE, 128), bf16),
+            vmem((EDGE, 128), bf16),
+            vmem((2 * STATE + 8, 128), f32),
+            vmem(((N + 1) * 2 * STATE, 128), f32),
+            vmem((STATE + 8, 128), f32),
             vmem((CHIPS * STATE, 128), f32),
             vmem((ROWS, D), f32),
-            vmem((ROWS * 32, 128), f32),
-            vmem((ROWS * 32, 128), f32),
+            vmem(((ROWS + 1) * 32, 128), f32),
+            vmem(((ROWS + 1) * 32, 128), f32),
             vmem((3, ROWS + 8, 128), f32),
-            vmem((N * STATE, 128), f32),
-            vmem((CHIPS * STATE, 128), f32),
-            vmem((CHIPS * STATE, 128), f32),
-            vmem((CHIPS * STATE, 128), f32),
-            vmem((CHIPS * STATE, 128), f32),
-            vmem((CHIPS * STATE, 128), f32),
-            vmem((CHIPS * STATE, 128), f32),
-            vmem((N * STATE, 128), f32),
+            vmem(((N + 1) * STATE, 128), f32),
+            vmem((CHIPS * STATE, 128), f32),
+            vmem((CHIPS * STATE, 128), f32),
+            vmem((CHIPS * STATE, 128), f32),
+            vmem((CHIPS * STATE, 128), f32),
+            vmem((CHIPS * STATE, 128), f32),
+            vmem((CHIPS * STATE, 128), f32),
+            vmem(((N + 1) * STATE, 128), f32),
             vmem((HEADS, 3, SEQ, HEAD), bf16),
             vmem((SEQ, SEQ), bf16),
             vmem((SEQ, HEAD), f32),

time: 63.9 us -> 63.9 us (level)
  no operation moved by 1% of the time
where the time goes in v5:
time: 63.9 us; the launch traced here: 63.7 us
  Pallas kernels  63 us (99%)
  between operations  0.64 us (1%)
    pallas_call x1, Pallas kernels, local(): pl.pallas_call(kernel, out_shape=(result, result), in_specs=[hbm] * 9, ou...  60.6 us
    pallas_call x1, Pallas kernels, local(): pl.pallas_call(hand_over, out_shape=(result, result), in_specs=[hbm, hbm]...  2.4 us

profile of v5, /device:TPU:1, one launch (start us, length us, event | category | flops | bytes accessed | tf_op | source)
XLA Modules:
  0.0 63.7 jit_solution(5239844099026425809)
XLA Ops:
  0.6 60.6 %shard_map.104 = (bf16[128,4096]{1,0:T(8,128)(2,1)}, bf16[128,4096]{1,0:T(8,128)(2,1)}) custom-call(bf16[128,4096]{1,0:T(8,128)(2,1)} %hq.1, bf16[128,4096]{1,0:T(8,128)(2,1)} %hk.1, bf16[128,4096]{1,0:T(8,128)(2,1)} %hv.1, f32[3,3,4096]{2,1,0:T(4,128)} %taps_in.1, f32[16,256]{1,0:T(8,128)} %bitcast.2, f32[16,256]{1,0:T(8,128)} %bitcast.3, ...), custom_call_target="tpu_custom_call" | custom-call | tf_op jit(solution)/shard_map/pallas_call | solution.py:418
  61.3 2.4 %shard_map.105 = (bf16[128,4096]{1,0:T(8,128)(2,1)}, bf16[128,4096]{1,0:T(8,128)(2,1)}) custom-call(bf16[128,4096]{1,0:T(8,128)(2,1)} %get-tuple-element.4.a_in, bf16[128,4096]{1,0:T(8,128)(2,1)} %get-tuple-element.5.b_in), custom_call_target="tpu_custom_call" | custom-call | tf_op jit(solution)/shard_map/pallas_call | solution.py:472

commit v6 on v5

--- a/solution.py
+++ b/solution.py
@@ -235,10 +235,6 @@
         leap[pl.ds(half, MODES, stride=2), :] = jnp.exp(-(rate[:, cs] * float(2 * ROWS)))
     slot = core * CHIPS + chip
     params[rows(slot, 2 * STATE), :] = mine[: 2 * STATE, :]
-    loads[2].wait()
-    all_in(hx, load_sem.at[3])
-    pack_edge(hx, wide)
-    edge[...] = wide[:EDGE, :].astype(bf16)
 
     pl.semaphore_wait(barrier, NEAR - 1)
     pl.semaphore_signal(ready, inc=1, device_id={"ctx": target(N // 2)}, device_id_type=MESH)
@@ -289,6 +285,10 @@
 
     each_chip(lambda d: par_copy(d, me).start(), 1, CHIPS // 2 + 1)
     qkv_start(0, (0,), end=NEAR)
+    loads[2].wait()
+    all_in(hx, load_sem.at[3])
+    pack_edge(hx, wide)
+    edge[...] = wide[:EDGE, :].astype(bf16)
     pl.semaphore_wait(ready, 1)
     each_chip(lambda d: par_copy(d, me).start(), CHIPS // 2 + 1, CHIPS)
 

time: 63.9 us -> 63.4 us (level)
  no operation moved by 1% of the time
where the time goes in v6:
time: 63.4 us; the launch traced here: 63.2 us
  Pallas kernels  62.6 us (99%)
  between operations  0.64 us (1%)
    pallas_call x1, Pallas kernels, local(): pl.pallas_call(kernel, out_shape=(result, result), in_specs=[hbm] * 9, ou...  60.2 us
    pallas_call x1, Pallas kernels, local(): pl.pallas_call(hand_over, out_shape=(result, result), in_specs=[hbm, hbm]...  2.4 us

profile of v6, /device:TPU:1, one launch (start us, length us, event | category | flops | bytes accessed | tf_op | source)
XLA Modules:
  0.0 63.2 jit_solution(9977572430531244797)
XLA Ops:
  0.6 60.2 %shard_map.104 = (bf16[128,4096]{1,0:T(8,128)(2,1)}, bf16[128,4096]{1,0:T(8,128)(2,1)}) custom-call(bf16[128,4096]{1,0:T(8,128)(2,1)} %hq.1, bf16[128,4096]{1,0:T(8,128)(2,1)} %hk.1, bf16[128,4096]{1,0:T(8,128)(2,1)} %hv.1, f32[3,3,4096]{2,1,0:T(4,128)} %taps_in.1, f32[16,256]{1,0:T(8,128)} %bitcast.2, f32[16,256]{1,0:T(8,128)} %bitcast.3, ...), custom_call_target="tpu_custom_call" | custom-call | tf_op jit(solution)/shard_map/pallas_call | solution.py:418
  60.8 2.4 %shard_map.105 = (bf16[128,4096]{1,0:T(8,128)(2,1)}, bf16[128,4096]{1,0:T(8,128)(2,1)}) custom-call(bf16[128,4096]{1,0:T(8,128)(2,1)} %get-tuple-element.4.a_in, bf16[128,4096]{1,0:T(8,128)(2,1)} %get-tuple-element.5.b_in), custom_call_target="tpu_custom_call" | custom-call | tf_op jit(solution)/shard_map/pallas_call | solution.py:472
